TPU v7x, 32 devices: a whole 2x2x4 slice. The times are simulated.
32 devices in a mesh: gx: 8 (over y, x, core), yz: 4 (over z).
Axes of the slice: x: 2, y: 2, z: 4, core: 2. Of those that a mesh axis runs over, the one named last changes fastest.
Arguments:
- design: float32 [32, 64, 128], P('gx', 'yz'), may hold values from 0.2 to 1
- passive: int32 [32, 64, 128], P('gx', 'yz'), may hold values 0 or 1
- support: int32 [32, 64, 128], P('gx', 'yz'), may hold values 0 or 1
- warm_modes: float32 [3, 12, 32, 64, 128], P(None, None, 'gx', 'yz'), may hold values from -6 to 6
Outputs:
- mode_shapes: float32 [3, 12, 32, 64, 128], P(None, None, 'gx', 'yz')
- projected: float32 [12, 12], replicated
All inputs are finite; a program needn't handle non-finite values. No bound on the sum of `passive` or of `support` on one device may be relied on, other than what follows from the above.
Results may differ from a plain program's by a relative error of at most 0.0001.
Values sent between devices are 32-bit elements; how exact they have to be, the bound alone decides.
A program may use at most 128 MiB of HBM per device.

v0:
```python
import jax
import jax.numpy as jnp
import numpy as np
from jax import lax
from jax.sharding import PartitionSpec as P

SWEEPS = 4


soft_modulus = 0.001
filter_weight = 2.0
cut_ratio = 0.02
highest_precision = lax.Precision.HIGHEST


def from_behind(value, axis, steps):
    count = lax.axis_size(axis)
    initial, last = (max(0, -steps), min(count, count - steps))
    return lax.ppermute(value, axis, [(source, source + steps) for source in range(initial, last)])


def with_halo(x, sides, width):
    for axis, dim in sides:
        devices, length = (lax.axis_size(axis), x.shape[dim])
        up = [(i, (i + 1) % devices) for i in range(devices - 1)]
        down = [(j, i) for i, j in up]
        last = lax.slice_in_dim(x, length - width, length, axis=dim)
        initial = lax.slice_in_dim(x, 0, width, axis=dim)
        before = lax.ppermute(last, axis, up)
        after = lax.ppermute(initial, axis, down)
        x = jnp.concatenate([before, x, after], axis=dim)
    return x


def element_matrix():
    poisson = 0.3
    lame_first = poisson / ((1.0 + poisson) * (1.0 - 2.0 * poisson))
    lame_shear = 0.5 / (1.0 + poisson)
    elastic = np.zeros((6, 6))
    elastic[:3, :3] = lame_first
    for direction in range(3):
        elastic[direction, direction] += 2.0 * lame_shear
        elastic[direction + 3, direction + 3] = lame_shear
    corner_signs = (
        np.array(
            [
                [a_side, b_side, c_side]
                for a_side in (0, 1)
                for b_side in (0, 1)
                for c_side in (0, 1)
            ]
        )
        * 2.0
        - 1.0
    )
    gauss_points = np.array([-1.0, 1.0]) / np.sqrt(3.0)
    stiffness = np.zeros((24, 24))
    for first_point in gauss_points:
        for second_point in gauss_points:
            for third_point in gauss_points:
                natural = np.array([first_point, second_point, third_point])
                gradients = np.zeros((8, 3))
                for corner in range(8):
                    for direction in range(3):
                        product = corner_signs[corner, direction] / 8.0
                        for other in range(3):
                            if other != direction:
                                product = product * (
                                    1.0 + corner_signs[corner, other] * natural[other]
                                )
                        gradients[corner, direction] = 2.0 * product
                strain = np.zeros((6, 24))
                for corner in range(8):
                    strain[0, corner] = gradients[corner, 0]
                    strain[1, 8 + corner] = gradients[corner, 1]
                    strain[2, 16 + corner] = gradients[corner, 2]
                    strain[3, corner] = gradients[corner, 1]
                    strain[3, 8 + corner] = gradients[corner, 0]
                    strain[4, 8 + corner] = gradients[corner, 2]
                    strain[4, 16 + corner] = gradients[corner, 1]
                    strain[5, corner] = gradients[corner, 2]
                    strain[5, 16 + corner] = gradients[corner, 0]
                stiffness = stiffness + strain.T @ elastic @ strain * 0.125
    return stiffness


def upper_value():
    return 8.0 * float(np.max(np.sum(np.abs(element_matrix()), axis=1)))


def jacobi(extended, design, neighbours, inside):
    padded = jnp.pad(extended, ((0, 0), (0, 0), (1, 1)))
    beside_all = padded[2:, 1:-1, 1:-1] + padded[:-2, 1:-1, 1:-1]
    beside_all = beside_all + padded[1:-1, 2:, 1:-1] + padded[1:-1, :-2, 1:-1]
    beside_all = beside_all + padded[1:-1, 1:-1, 2:] + padded[1:-1, 1:-1, :-2]
    return inside * (design + filter_weight * beside_all) / (1.0 + filter_weight * neighbours)


def neighbour_count(x_global, y_global, depth, x_total, y_total):
    z_global = jnp.arange(depth)
    x_part = (x_global > 0).astype(jnp.float32) + (x_global < x_total - 1).astype(jnp.float32)
    y_part = (y_global > 0).astype(jnp.float32) + (y_global < y_total - 1).astype(jnp.float32)
    z_part = (z_global > 0).astype(jnp.float32) + (z_global < depth - 1).astype(jnp.float32)
    return x_part[:, None, None] + y_part[None, :, None] + z_part[None, None, :]


def nodal_mass(density_ext, x_cells, y_cells, z_cells):
    lumped = jnp.zeros((x_cells, y_cells, z_cells), jnp.float32)
    for x_side in (0, 1):
        for y_side in (0, 1):
            for z_side in (0, 1):
                lumped = (
                    lumped
                    + density_ext[
                        1 - x_side : 1 - x_side + x_cells,
                        1 - y_side : 1 - y_side + y_cells,
                        1 - z_side : 1 - z_side + z_cells,
                    ]
                )
    return lumped / 8.0


def node_forces(node_block, moduli):
    stiffness = jnp.asarray(element_matrix(), jnp.float32)
    planes = moduli.shape[0]
    y_cells = moduli.shape[1]
    z_cells = moduli.shape[2]
    columns = node_block.shape[1]

    def add_plane(plane_index, accumulated):
        slab_plane = lax.dynamic_slice_in_dim(node_block, plane_index, 2, axis=2)
        corner_list = []
        for x_side in (0, 1):
            for y_side in (0, 1):
                for z_side in (0, 1):
                    corner_list.append(
                        slab_plane[
                            :, :, x_side, y_side : y_side + y_cells, z_side : z_side + z_cells
                        ]
                    )
        gathered = jnp.stack(corner_list, axis=1).reshape(24, columns, y_cells, z_cells)
        plane_moduli = lax.dynamic_index_in_dim(moduli, plane_index, 0, keepdims=False)
        element_force = (
            jnp.einsum("ab,bmyz->amyz", stiffness, gathered, precision=highest_precision)
            * plane_moduli
        )
        element_force = element_force.reshape(3, 8, columns, y_cells, z_cells)
        for x_side in (0, 1):
            spread = jnp.zeros((3, columns, y_cells + 1, z_cells + 1), jnp.float32)
            for y_side in (0, 1):
                for z_side in (0, 1):
                    corner = 4 * x_side + 2 * y_side + z_side
                    spread = spread + jnp.pad(
                        element_force[:, corner],
                        ((0, 0), (0, 0), (y_side, 1 - y_side), (z_side, 1 - z_side)),
                    )
            current = lax.dynamic_slice_in_dim(accumulated, plane_index + x_side, 1, axis=2)
            accumulated = lax.dynamic_update_slice_in_dim(
                accumulated, current + spread[:, :, None], plane_index + x_side, axis=2
            )
        return accumulated

    return lax.fori_loop(0, planes, add_plane, jnp.zeros(node_block.shape, jnp.float32))


def apply_operator(vectors, scaling, moduli_ext):
    scaled = scaling * vectors
    upper_plane = from_behind(scaled[:, :, :1], "gx", -1)
    with_plane = jnp.concatenate([scaled, upper_plane], axis=2)
    upper_column = from_behind(with_plane[:, :, :, :1], "yz", -1)
    node_block = jnp.concatenate([with_plane, upper_column], axis=3)
    node_block = jnp.pad(node_block, ((0, 0), (0, 0), (0, 0), (0, 0), (0, 1)))
    forces = node_forces(node_block, moduli_ext[1:, 1:, 1:])
    forces = forces[:, :, :, :, :-1]
    column_back = from_behind(forces[:, :, :, -1:], "yz", 1)
    forces = jnp.concatenate([forces[:, :, :, :1] + column_back, forces[:, :, :, 1:-1]], axis=3)
    plane_back = from_behind(forces[:, :, -1:], "gx", 1)
    forces = jnp.concatenate([forces[:, :, :1] + plane_back, forces[:, :, 1:-1]], axis=2)
    return scaling * forces


def on_device(design, passive, support, warm_modes):
    x_cells, y_cells, z_cells = design.shape
    x_total = x_cells * lax.axis_size("gx")
    y_total = y_cells * lax.axis_size("yz")
    x_start = lax.axis_index("gx") * x_cells
    y_start = lax.axis_index("yz") * y_cells
    neighbours = neighbour_count(
        x_start + jnp.arange(x_cells), y_start + jnp.arange(y_cells), z_cells, x_total, y_total
    )
    filtered = design
    for sweep_index in range(SWEEPS):
        extended = with_halo(filtered, (("gx", 0), ("yz", 1)), 1)
        filtered = jacobi(extended, design, neighbours, 1.0)
    density = jnp.where(passive == 1, jnp.float32(1.0), filtered)
    moduli = soft_modulus + (1.0 - soft_modulus) * density**3
    paired = jnp.stack([density, moduli])
    below_plane = from_behind(paired[:, -1:], "gx", 1)
    paired = jnp.concatenate([below_plane, paired], axis=1)
    below_column = from_behind(paired[:, :, -1:], "yz", 1)
    paired = jnp.concatenate([below_column, paired], axis=2)
    paired = jnp.pad(paired, ((0, 0), (0, 0), (0, 0), (1, 0)))
    density_ext = paired[0]
    moduli_ext = paired[1]
    lumped = nodal_mass(density_ext, x_cells, y_cells, z_cells)
    scaling = (1.0 - support.astype(jnp.float32)) / jnp.sqrt(lumped)
    upper_edge = upper_value()
    lower_edge = cut_ratio * upper_edge
    center_value = 0.5 * (upper_edge + lower_edge)
    half_width = 0.5 * (upper_edge - lower_edge)
    previous = warm_modes * (1.0 - support.astype(jnp.float32))
    latest = (apply_operator(previous, scaling, moduli_ext) - center_value * previous) / half_width
    following = (
        2.0 * (apply_operator(latest, scaling, moduli_ext) - center_value * latest) / half_width
        - previous
    )
    image = apply_operator(following, scaling, moduli_ext)
    total_dof = 3.0 * x_total * y_total * z_cells
    gram_part = (
        jnp.einsum("cixyz,cjxyz->ij", following, following, precision=highest_precision) / total_dof
    )
    stiff_part = (
        jnp.einsum("cixyz,cjxyz->ij", following, image, precision=highest_precision) / total_dof
    )
    gram, stiff = lax.psum((gram_part, stiff_part), ("gx", "yz"))
    lower = jnp.linalg.cholesky(gram)
    inverse = jax.scipy.linalg.solve_triangular(
        lower, jnp.eye(gram.shape[0], dtype=jnp.float32), lower=True
    )
    ortho = jnp.einsum("ji,cixyz->cjxyz", inverse, following, precision=highest_precision)
    projected = jnp.dot(
        jnp.dot(inverse, stiff, precision=highest_precision), inverse.T, precision=highest_precision
    )
    return (scaling * ortho, projected)


def solution(mesh):
    return jax.shard_map(
        on_device,
        mesh=mesh,
        in_specs=(
            P("gx", "yz", None),
            P("gx", "yz", None),
            P("gx", "yz", None),
            P(None, None, "gx", "yz", None),
        ),
        out_specs=(P(None, None, "gx", "yz", None), P()),
        check_vma=False,
    )
```

profile of v0, /device:TPU:0, one launch (start us, length us, event | category | flops | bytes accessed | tf_op | source)
XLA Modules:
  0.0 527.2 jit_solution(9451657886428057653)
XLA Ops:
  6.0 3.0 collective-permute-done
  10.3 4.5 collective-permute-start.3
  18.6 3.8 collective-permute-start.5
  24.5 4.5 collective-permute-start.7
  32.6 3.3 collective-permute-start.9
  38.1 4.5 collective-permute-start.11
  46.3 5.1 collective-permute-start.13
  53.4 4.5 collective-permute-start.15
  60.3 4.4 collective-permute-start.16
  65.6 3.9 collective-permute-start.17
  74.1 4.4 collective-permute-done.18
  80.1 5.2 collective-permute-done.19
  90.3 89.7 %while.48 = (s32[]{:T(128)}, f32[3,12,5,17,129]{4,0,3,1,2:T(4,128)}, f32[3,12,5,17,129]{4,0,3,1,2:T(4,128)}, f32[4,16,128]{2,1,0:T(8,128)S(1)}, s32[]{:T(128)}, ...) while((s32[]{:T(128)}, f32[3,12,5,17,129]{4,0,3,1,2:T(4,128)}, ...), condition=%wide.region_1.2_spmd.clone, body=%wide.region_0.1_spmd.sunk.clone.sunk | while | flops 171090720 | bytes 25389536 | solution.py:163
  100.8 3.4 multiply_bitcast_fusion.7
  123.2 3.4 multiply_bitcast_fusion.7
  145.6 3.4 multiply_bitcast_fusion.7
  154.4 3.0 fusion.199
  168.0 3.4 multiply_bitcast_fusion.7
  173.5 3.0 fusion.198
  176.9 3.0 fusion.199
  180.9 3.9 collective-permute-start.20
  188.8 7.7 %collective-permute-start.21 = (f32[3,12,1,16,128]{4,0,3,1,2:T(4,128)S(1)}, f32[3,12,1,16,128]{4,0,3,1,2:T(4,128)S(1)}, u32[]{:S(2)}, u32[]{:S(2)}) collective-permute-start(f32[3,12,1,16,128]{4,0,3,1,2:T(4,128)S(1)} %pad_maximum_fusion.2), channel_id=1, source_target_pairs={{0,4},{4,8},{8,12},{12,16},{16,20},{20,24},{24,28},{1,5},{5,9},{9,... | collective-permute-start | bytes 884744 | tf_op jit(solution)/shard_map/ppermute | solution.py:19
  200.7 6.9 %collective-permute-done.22 = f32[3,12,1,16,128]{4,0,3,1,2:T(4,128)S(1)} collective-permute-done((f32[3,12,1,16,128]{4,0,3,1,2:T(4,128)S(1)}, f32[3,12,1,16,128]{4,0,3,1,2:T(4,128)S(1)}, u32[]{:S(2)}, u32[]{:S(2)}) %collective-permute-start.22) | collective-permute-done | bytes 294944 | tf_op jit(solution)/shard_map/ppermute | solution.py:19
  209.1 5.3 collective-permute-done.23
  219.3 94.9 %while.49 = (s32[]{:T(128)}, f32[3,12,5,17,129]{4,0,3,1,2:T(4,128)}, f32[3,12,5,17,129]{4,0,3,1,2:T(4,128)}, f32[4,16,128]{2,1,0:T(8,128)S(1)}, s32[]{:T(128)}, ...) while((s32[]{:T(128)}, f32[3,12,5,17,129]{4,0,3,1,2:T(4,128)}, ...), condition=%wide.region_3.4_spmd.clone, body=%wide.region_2.3_spmd.sunk.clone.sunk | while | flops 171090720 | bytes 25651736 | solution.py:163
  231.2 3.4 multiply_bitcast_fusion.8
  254.9 3.4 multiply_bitcast_fusion.8
  278.5 3.4 multiply_bitcast_fusion.8
  287.4 3.0 fusion.212
  302.2 3.4 multiply_bitcast_fusion.8
  307.7 3.0 fusion.211
  311.2 3.0 fusion.212
  315.1 3.9 collective-permute-start.24
  322.8 7.0 %collective-permute-start.25 = (f32[3,12,1,16,128]{4,0,3,1,2:T(4,128)S(1)}, f32[3,12,1,16,128]{4,0,3,1,2:T(4,128)S(1)}, u32[]{:S(2)}, u32[]{:S(2)}) collective-permute-start(f32[3,12,1,16,128]{4,0,3,1,2:T(4,128)S(1)} %pad_maximum_fusion.1), channel_id=1, source_target_pairs={{0,4},{4,8},{8,12},{12,16},{16,20},{20,24},{24,28},{1,5},{5,9},{9,... | collective-permute-start | bytes 884744 | tf_op jit(solution)/shard_map/ppermute | solution.py:19
  335.6 7.1 %collective-permute-done.26 = f32[3,12,1,16,128]{4,0,3,1,2:T(4,128)S(1)} collective-permute-done((f32[3,12,1,16,128]{4,0,3,1,2:T(4,128)S(1)}, f32[3,12,1,16,128]{4,0,3,1,2:T(4,128)S(1)}, u32[]{:S(2)}, u32[]{:S(2)}) %collective-permute-start.26) | collective-permute-done | bytes 294944 | tf_op jit(solution)/shard_map/ppermute | solution.py:19
  344.4 5.2 collective-permute-done.27
  354.6 89.7 %while.50 = (s32[]{:T(128)}, f32[3,12,5,17,129]{4,0,3,1,2:T(4,128)}, f32[3,12,5,17,129]{4,0,3,1,2:T(4,128)}, f32[4,16,128]{2,1,0:T(8,128)S(1)}, s32[]{:T(128)}, ...) while((s32[]{:T(128)}, f32[3,12,5,17,129]{4,0,3,1,2:T(4,128)}, ...), condition=%wide.region_8.9_spmd.clone, body=%wide.region_7.8_spmd.sunk.clone.sunk | while | flops 171090720 | bytes 25389536 | solution.py:163
  365.1 3.4 multiply_bitcast_fusion.9
  387.5 3.4 multiply_bitcast_fusion.9
  409.8 3.4 multiply_bitcast_fusion.9
  418.7 3.0 fusion.225
  432.3 3.4 multiply_bitcast_fusion.9
  437.8 3.0 fusion.224
  441.2 3.0 fusion.225
  445.2 4.1 collective-permute-start.28
  452.7 7.3 %collective-permute-start.29 = (f32[3,12,1,16,128]{4,0,3,1,2:T(4,128)S(1)}, f32[3,12,1,16,128]{4,0,3,1,2:T(4,128)S(1)}, u32[]{:S(2)}, u32[]{:S(2)}) collective-permute-start(f32[3,12,1,16,128]{4,0,3,1,2:T(4,128)S(1)} %pad_maximum_fusion), channel_id=1, source_target_pairs={{0,4},{4,8},{8,12},{12,16},{16,20},{20,24},{24,28},{1,5},{5,9},{9,... | collective-permute-start | bytes 884744 | tf_op jit(solution)/shard_map/ppermute | solution.py:19
  463.2 3.1 fusion.75
  466.3 52.3 %all-reduce.32 = (f32[12,12]{0,1:T(8,128)S(1)}, f32[12,12]{0,1:T(8,128)S(1)}) all-reduce(f32[12,12]{0,1:T(8,128)S(1)} %fusion.80, f32[12,12]{0,1:T(8,128)S(1)} %fusion.75), channel_id=1, replica_groups=mesh['gx'=8,'yz'=4] {'gx','yz'}, use_global_device_ids=true, to_apply=%region_4.5 | all-reduce | flops 288 | bytes 2304 | tf_op jit(solution)/shard_map/psum | solution.py:225
  (340 shorter events, 290.4 us)
Async XLA Ops:
  0.6 71.3 %copy-start.3 = (f32[3,12,4,16,128]{4,3,2,1,0:T(8,128)S(1)}, f32[3,12,4,16,128]{4,3,2,1,0:T(8,128)}, u32[]{:S(2)}) copy-start(f32[3,12,4,16,128]{4,3,2,1,0:T(8,128)} %param.16) | copy-start | bytes 3538948
  1.5 3.8 collective-permute-start.1
  3.8 5.2 collective-permute-start
  9.0 5.9 %collective-permute-start.2 = (f32[6,1,128]{2,1,0:T(1,128)S(1)}, f32[6,1,128]{2,1,0:T(1,128)S(1)}, u32[]{:S(2)}, u32[]{:S(2)}) collective-permute-start(f32[6,1,128]{2,1,0:T(1,128)S(1)} %get-tuple-element.540), channel_id=1, source_target_pairs={{1,0},{2,1},{3,2},{5,4},{6,5},{7,6},{9,8},{10,9},{11,10},{13,12},{... | collective-permute-start | bytes 9224 | tf_op jit(solution)/shard_map/ppermute | solution.py:30
  10.3 5.9 %collective-permute-start.3 = (f32[6,1,128]{2,1,0:T(1,128)S(1)}, f32[6,1,128]{2,1,0:T(1,128)S(1)}, u32[]{:S(2)}, u32[]{:S(2)}) collective-permute-start(f32[6,1,128]{2,1,0:T(1,128)S(1)} %get-tuple-element.539), channel_id=1, source_target_pairs={{0,1},{1,2},{2,3},{4,5},{5,6},{6,7},{8,9},{9,10},{10,11},{12,13},{... | collective-permute-start | bytes 9224 | tf_op jit(solution)/shard_map/ppermute | solution.py:29
  17.3 5.1 collective-permute-start.4
  18.6 4.6 collective-permute-start.5
  23.2 5.8 %collective-permute-start.6 = (f32[6,1,128]{2,1,0:T(1,128)S(1)}, f32[6,1,128]{2,1,0:T(1,128)S(1)}, u32[]{:S(2)}, u32[]{:S(2)}) collective-permute-start(f32[6,1,128]{2,1,0:T(1,128)S(1)} %get-tuple-element.538), channel_id=1, source_target_pairs={{1,0},{2,1},{3,2},{5,4},{6,5},{7,6},{9,8},{10,9},{11,10},{13,12},{... | collective-permute-start | bytes 9224 | tf_op jit(solution)/shard_map/ppermute | solution.py:30
  24.5 5.9 %collective-permute-start.7 = (f32[6,1,128]{2,1,0:T(1,128)S(1)}, f32[6,1,128]{2,1,0:T(1,128)S(1)}, u32[]{:S(2)}, u32[]{:S(2)}) collective-permute-start(f32[6,1,128]{2,1,0:T(1,128)S(1)} %get-tuple-element.537), channel_id=1, source_target_pairs={{0,1},{1,2},{2,3},{4,5},{5,6},{6,7},{8,9},{9,10},{10,11},{12,13},{... | collective-permute-start | bytes 9224 | tf_op jit(solution)/shard_map/ppermute | solution.py:29
  31.3 4.7 collective-permute-start.8
  32.6 4.2 collective-permute-start.9
  36.8 5.8 %collective-permute-start.10 = (f32[6,1,128]{2,1,0:T(1,128)S(1)}, f32[6,1,128]{2,1,0:T(1,128)S(1)}, u32[]{:S(2)}, u32[]{:S(2)}) collective-permute-start(f32[6,1,128]{2,1,0:T(1,128)S(1)} %get-tuple-element.536), channel_id=1, source_target_pairs={{1,0},{2,1},{3,2},{5,4},{6,5},{7,6},{9,8},{10,9},{11,10},{13,12},{... | collective-permute-start | bytes 9224 | tf_op jit(solution)/shard_map/ppermute | solution.py:30
  38.1 5.9 %collective-permute-start.11 = (f32[6,1,128]{2,1,0:T(1,128)S(1)}, f32[6,1,128]{2,1,0:T(1,128)S(1)}, u32[]{:S(2)}, u32[]{:S(2)}) collective-permute-start(f32[6,1,128]{2,1,0:T(1,128)S(1)} %get-tuple-element.535), channel_id=1, source_target_pairs={{0,1},{1,2},{2,3},{4,5},{5,6},{6,7},{8,9},{9,10},{10,11},{12,13},{... | collective-permute-start | bytes 9224 | tf_op jit(solution)/shard_map/ppermute | solution.py:29
  45.0 6.4 %collective-permute-start.12 = (f32[1,16,128]{2,1,0:T(8,128)S(1)}, f32[1,16,128]{2,1,0:T(8,128)S(1)}, u32[]{:S(2)}, u32[]{:S(2)}) collective-permute-start(f32[1,16,128]{2,1,0:T(8,128)S(1)} %get-tuple-element.543), channel_id=1, source_target_pairs={{4,0},{8,4},{12,8},{16,12},{20,16},{24,20},{28,24},{5,1},{9,5},{13... | collective-permute-start | bytes 24584 | tf_op jit(solution)/shard_map/ppermute | solution.py:30
  46.3 5.9 %collective-permute-start.13 = (f32[1,16,128]{2,1,0:T(8,128)S(1)}, f32[1,16,128]{2,1,0:T(8,128)S(1)}, u32[]{:S(2)}, u32[]{:S(2)}) collective-permute-start(f32[1,16,128]{2,1,0:T(8,128)S(1)} %get-tuple-element.542), channel_id=1, source_target_pairs={{0,4},{4,8},{8,12},{12,16},{16,20},{20,24},{24,28},{1,5},{5,9},{9,... | collective-permute-start | bytes 24584 | tf_op jit(solution)/shard_map/ppermute | solution.py:29
  52.2 5.8 %collective-permute-start.14 = (f32[6,1,128]{2,1,0:T(1,128)S(1)}, f32[6,1,128]{2,1,0:T(1,128)S(1)}, u32[]{:S(2)}, u32[]{:S(2)}) collective-permute-start(f32[6,1,128]{2,1,0:T(1,128)S(1)} %get-tuple-element.534), channel_id=1, source_target_pairs={{1,0},{2,1},{3,2},{5,4},{6,5},{7,6},{9,8},{10,9},{11,10},{13,12},{... | collective-permute-start | bytes 9224 | tf_op jit(solution)/shard_map/ppermute | solution.py:30
  53.4 5.9 %collective-permute-start.15 = (f32[6,1,128]{2,1,0:T(1,128)S(1)}, f32[6,1,128]{2,1,0:T(1,128)S(1)}, u32[]{:S(2)}, u32[]{:S(2)}) collective-permute-start(f32[6,1,128]{2,1,0:T(1,128)S(1)} %get-tuple-element.533), channel_id=1, source_target_pairs={{0,1},{1,2},{2,3},{4,5},{5,6},{6,7},{8,9},{9,10},{10,11},{12,13},{... | collective-permute-start | bytes 9224 | tf_op jit(solution)/shard_map/ppermute | solution.py:29
  60.3 5.2 collective-permute-start.16
  65.6 5.2 collective-permute-start.17
  71.9 6.7 %copy-start.9 = (f32[4,16,128]{2,1,0:T(8,128)}, f32[4,16,128]{2,1,0:T(8,128)S(1)}, u32[]{:S(2)}) copy-start(f32[4,16,128]{2,1,0:T(8,128)S(1)} %get-tuple-element.480) | copy-start | bytes 98308
  71.9 126.1 %copy-start.15 = (f32[4,16,128]{2,1,0:T(8,128)}, f32[4,16,128]{2,1,0:T(8,128)S(1)}, u32[]{:S(2)}) copy-start(f32[4,16,128]{2,1,0:T(8,128)S(1)} %get-tuple-element.541) | copy-start | bytes 98308
  72.8 5.7 %collective-permute-start.18 = (f32[3,12,1,16,128]{4,0,3,1,2:T(4,128)S(1)}, f32[3,12,1,16,128]{4,0,3,1,2:T(4,128)S(1)}, u32[]{:S(2)}, u32[]{:S(2)}) collective-permute-start(f32[3,12,1,16,128]{4,0,3,1,2:T(4,128)S(1)} %slice.999), channel_id=1, source_target_pairs={{4,0},{8,4},{12,8},{16,12},{20,16},{24,20},{28,24},{5,1},{9,5},{13... | collective-permute-start | bytes 884744 | tf_op jit(solution)/shard_map/ppermute | solution.py:19
  78.6 6.8 %collective-permute-start.19 = (f32[3,12,5,1,128]{4,0,3,1,2:T(4,128)S(1)}, f32[3,12,5,1,128]{4,0,3,1,2:T(4,128)S(1)}, u32[]{:S(2)}, u32[]{:S(2)}) collective-permute-start(f32[3,12,5,1,128]{4,0,3,1,2:T(4,128)S(1)} %pad_maximum_fusion.5), channel_id=1, source_target_pairs={{1,0},{2,1},{3,2},{5,4},{6,5},{7,6},{9,8},{10,9},{11,10},{13,12},{... | collective-permute-start | bytes 276488 | tf_op jit(solution)/shard_map/ppermute | solution.py:19
  180.9 6.3 %collective-permute-start.20 = (f32[3,12,5,1,128]{4,0,3,1,2:T(4,128)S(1)}, f32[3,12,5,1,128]{4,0,3,1,2:T(4,128)S(1)}, u32[]{:S(2)}, u32[]{:S(2)}) collective-permute-start(f32[3,12,5,1,128]{4,0,3,1,2:T(4,128)S(1)} %slice.833), channel_id=1, source_target_pairs={{0,1},{1,2},{2,3},{4,5},{5,6},{6,7},{8,9},{9,10},{10,11},{12,13},{... | collective-permute-start | bytes 276488 | tf_op jit(solution)/shard_map/ppermute | solution.py:19
  186.6 12.6 %copy-start = (f32[3,12,5,15,128]{4,0,3,1,2:T(4,128)}, f32[3,12,5,15,128]{4,0,3,1,2:T(4,128)S(1)}, u32[]{:S(2)}) copy-start(f32[3,12,5,15,128]{4,0,3,1,2:T(4,128)S(1)} %slice.834) | copy-start | bytes 4147204
  186.6 11.3 %copy-start.4 = (f32[3,12,4,16,128]{4,3,2,1,0:T(8,128)S(1)}, f32[3,12,4,16,128]{4,3,2,1,0:T(8,128)}, u32[]{:S(2)}) copy-start(f32[3,12,4,16,128]{4,3,2,1,0:T(8,128)} %param.16) | copy-start | bytes 3538948
  186.7 11.3 %copy-start.10 = (f32[4,16,128]{2,1,0:T(8,128)S(1)}, f32[4,16,128]{2,1,0:T(8,128)}, u32[]{:S(2)}) copy-start(f32[4,16,128]{2,1,0:T(8,128)} %copy-done.9) | copy-start | bytes 98308
  188.6 10.6 %copy-start.6 = (f32[3,12,5,1,128]{4,0,3,1,2:T(4,128)}, f32[3,12,5,1,128]{4,0,3,1,2:T(4,128)S(1)}, u32[]{:S(2)}) copy-start(f32[3,12,5,1,128]{4,0,3,1,2:T(4,128)S(1)} %slice_add_fusion.2) | copy-start | bytes 276484
  188.8 9.0 %collective-permute-start.21 = (f32[3,12,1,16,128]{4,0,3,1,2:T(4,128)S(1)}, f32[3,12,1,16,128]{4,0,3,1,2:T(4,128)S(1)}, u32[]{:S(2)}, u32[]{:S(2)}) collective-permute-start(f32[3,12,1,16,128]{4,0,3,1,2:T(4,128)S(1)} %pad_maximum_fusion.2), channel_id=1, source_target_pairs={{0,4},{4,8},{8,12},{12,16},{16,20},{20,24},{24,28},{1,5},{5,9},{9,... | collective-permute-start | bytes 884744 | tf_op jit(solution)/shard_map/ppermute | solution.py:19
  199.4 8.2 %collective-permute-start.22 = (f32[3,12,1,16,128]{4,0,3,1,2:T(4,128)S(1)}, f32[3,12,1,16,128]{4,0,3,1,2:T(4,128)S(1)}, u32[]{:S(2)}, u32[]{:S(2)}) collective-permute-start(f32[3,12,1,16,128]{4,0,3,1,2:T(4,128)S(1)} %slice.1002), channel_id=1, source_target_pairs={{4,0},{8,4},{12,8},{16,12},{20,16},{24,20},{28,24},{5,1},{9,5},{13... | collective-permute-start | bytes 884744 | tf_op jit(solution)/shard_map/ppermute | solution.py:19
  207.6 6.8 %collective-permute-start.23 = (f32[3,12,5,1,128]{4,0,3,1,2:T(4,128)S(1)}, f32[3,12,5,1,128]{4,0,3,1,2:T(4,128)S(1)}, u32[]{:S(2)}, u32[]{:S(2)}) collective-permute-start(f32[3,12,5,1,128]{4,0,3,1,2:T(4,128)S(1)} %pad_maximum_fusion.4), channel_id=1, source_target_pairs={{1,0},{2,1},{3,2},{5,4},{6,5},{7,6},{9,8},{10,9},{11,10},{13,12},{... | collective-permute-start | bytes 276488 | tf_op jit(solution)/shard_map/ppermute | solution.py:19
  239.6 3.4 copy-start.14
  263.3 3.4 copy-start.14
  287.0 3.4 copy-start.14
  310.8 3.4 copy-start.14
  315.1 6.4 %collective-permute-start.24 = (f32[3,12,5,1,128]{4,0,3,1,2:T(4,128)S(1)}, f32[3,12,5,1,128]{4,0,3,1,2:T(4,128)S(1)}, u32[]{:S(2)}, u32[]{:S(2)}) collective-permute-start(f32[3,12,5,1,128]{4,0,3,1,2:T(4,128)S(1)} %slice.841), channel_id=1, source_target_pairs={{0,1},{1,2},{2,3},{4,5},{5,6},{6,7},{8,9},{9,10},{10,11},{12,13},{... | collective-permute-start | bytes 276488 | tf_op jit(solution)/shard_map/ppermute | solution.py:19
  320.9 10.4 %copy-start.1 = (f32[3,12,5,15,128]{4,0,3,1,2:T(4,128)S(1)}, f32[3,12,5,15,128]{4,0,3,1,2:T(4,128)}, u32[]{:S(2)}) copy-start(f32[3,12,5,15,128]{4,0,3,1,2:T(4,128)} %copy-done) | copy-start | bytes 4147204
  320.9 10.4 %copy-start.5 = (f32[3,12,4,16,128]{4,3,2,1,0:T(8,128)S(1)}, f32[3,12,4,16,128]{4,3,2,1,0:T(8,128)}, u32[]{:S(2)}) copy-start(f32[3,12,4,16,128]{4,3,2,1,0:T(8,128)} %param.16) | copy-start | bytes 3538948
  320.9 10.4 %copy-start.7 = (f32[3,12,5,1,128]{4,0,3,1,2:T(4,128)S(1)}, f32[3,12,5,1,128]{4,0,3,1,2:T(4,128)}, u32[]{:S(2)}) copy-start(f32[3,12,5,1,128]{4,0,3,1,2:T(4,128)} %copy-done.6) | copy-start | bytes 276484
  320.9 10.4 %copy-start.11 = (f32[4,16,128]{2,1,0:T(8,128)S(1)}, f32[4,16,128]{2,1,0:T(8,128)}, u32[]{:S(2)}) copy-start(f32[4,16,128]{2,1,0:T(8,128)} %copy-done.9) | copy-start | bytes 98308
  321.0 10.4 %copy-start.16 = (f32[4,16,128]{2,1,0:T(8,128)S(1)}, f32[4,16,128]{2,1,0:T(8,128)}, u32[]{:S(2)}) copy-start(f32[4,16,128]{2,1,0:T(8,128)} %copy-done.15) | copy-start | bytes 98308
  322.8 8.3 %collective-permute-start.25 = (f32[3,12,1,16,128]{4,0,3,1,2:T(4,128)S(1)}, f32[3,12,1,16,128]{4,0,3,1,2:T(4,128)S(1)}, u32[]{:S(2)}, u32[]{:S(2)}) collective-permute-start(f32[3,12,1,16,128]{4,0,3,1,2:T(4,128)S(1)} %pad_maximum_fusion.1), channel_id=1, source_target_pairs={{0,4},{4,8},{8,12},{12,16},{16,20},{20,24},{24,28},{1,5},{5,9},{9,... | collective-permute-start | bytes 884744 | tf_op jit(solution)/shard_map/ppermute | solution.py:19
  334.3 8.4 %collective-permute-start.26 = (f32[3,12,1,16,128]{4,0,3,1,2:T(4,128)S(1)}, f32[3,12,1,16,128]{4,0,3,1,2:T(4,128)S(1)}, u32[]{:S(2)}, u32[]{:S(2)}) collective-permute-start(f32[3,12,1,16,128]{4,0,3,1,2:T(4,128)S(1)} %slice.1003), channel_id=1, source_target_pairs={{4,0},{8,4},{12,8},{16,12},{20,16},{24,20},{28,24},{5,1},{9,5},{13... | collective-permute-start | bytes 884744 | tf_op jit(solution)/shard_map/ppermute | solution.py:19
  342.7 6.9 %collective-permute-start.27 = (f32[3,12,5,1,128]{4,0,3,1,2:T(4,128)S(1)}, f32[3,12,5,1,128]{4,0,3,1,2:T(4,128)S(1)}, u32[]{:S(2)}, u32[]{:S(2)}) collective-permute-start(f32[3,12,5,1,128]{4,0,3,1,2:T(4,128)S(1)} %pad_maximum_fusion.3), channel_id=1, source_target_pairs={{1,0},{2,1},{3,2},{5,4},{6,5},{7,6},{9,8},{10,9},{11,10},{13,12},{... | collective-permute-start | bytes 276488 | tf_op jit(solution)/shard_map/ppermute | solution.py:19
  445.2 14.8 %copy-start.2 = (f32[3,12,4,16,128]{4,0,3,1,2:T(4,128)S(1)}, f32[3,12,4,16,128]{4,0,3,1,2:T(4,128)}, u32[]{:S(2)}) copy-start(f32[3,12,4,16,128]{4,0,3,1,2:T(4,128)} %get-tuple-element.478) | copy-start | bytes 3538948
  445.2 6.5 %collective-permute-start.28 = (f32[3,12,5,1,128]{4,0,3,1,2:T(4,128)S(1)}, f32[3,12,5,1,128]{4,0,3,1,2:T(4,128)S(1)}, u32[]{:S(2)}, u32[]{:S(2)}) collective-permute-start(f32[3,12,5,1,128]{4,0,3,1,2:T(4,128)S(1)} %slice.849), channel_id=1, source_target_pairs={{0,1},{1,2},{2,3},{4,5},{5,6},{6,7},{8,9},{9,10},{10,11},{12,13},{... | collective-permute-start | bytes 276488 | tf_op jit(solution)/shard_map/ppermute | solution.py:19
  452.6 10.1 %copy-start.12 = (f32[4,16,128]{2,1,0:T(8,128)S(1)}, f32[4,16,128]{2,1,0:T(8,128)}, u32[]{:S(2)}) copy-start(f32[4,16,128]{2,1,0:T(8,128)} %copy-done.9) | copy-start | bytes 98308
  452.7 9.8 %collective-permute-start.29 = (f32[3,12,1,16,128]{4,0,3,1,2:T(4,128)S(1)}, f32[3,12,1,16,128]{4,0,3,1,2:T(4,128)S(1)}, u32[]{:S(2)}, u32[]{:S(2)}) collective-permute-start(f32[3,12,1,16,128]{4,0,3,1,2:T(4,128)S(1)} %pad_maximum_fusion), channel_id=1, source_target_pairs={{0,4},{4,8},{8,12},{12,16},{16,20},{20,24},{24,28},{1,5},{5,9},{9,... | collective-permute-start | bytes 884744 | tf_op jit(solution)/shard_map/ppermute | solution.py:19
  (5 other events, 5.0 us)
where the time goes:
time: 537 us; the launch traced here: 527 us
  local copies, waits for them, and re-layouts  179 us (33%)
  other arithmetic  97.1 us (18%)
  starting transfers between devices  93.8 us (17%)
  blocking collectives  52.3 us (10%)
  waiting for transfers between devices  51.1 us (10%)
  matrix products  50.6 us (9%)
    while x100, local copies, waits for them, and re-layouts  110 us
    dynamic_update_slice x24, other arithmetic, add_plane(): lax.dynamic_update_slice_in_dim(accumulated, current + spread[:, :, None]...  71.6 us
    psum x1, blocking collectives, on_device(): gram, stiff = lax.psum((gram_part, stiff_part), ('gx', 'yz'))  52.3 us
    ppermute x14, starting transfers between devices, from_behind(): lax.ppermute(value, axis, [(source, source + steps) for source in range(i...  50.7 us
    dot_general x12, matrix products, add_plane(): jnp.einsum('ab,bmyz->amyz', stiffness, gathered, precision=highest_precis...  41.4 us
    ppermute x14, waiting for transfers between devices, from_behind(): lax.ppermute(value, axis, [(source, source + steps) for source in range(i...  40.5 us
    ppermute x8, starting transfers between devices, with_halo(): before = lax.ppermute(last, axis, up)  32.8 us
    slice x12, local copies, waits for them, and re-layouts, add_plane(): element_force[:, corner]  19.5 us
  transfers between devices with their start and end apart: 30, of which 21 were waited for; matrix products, arithmetic and copies ran while one was open for 2% of the time, Pallas kernels for 0%

commit v1 on v0

v1 whole, which is shorter than its diff:
```python
import functools

import jax
import jax.numpy as jnp
import numpy as np
from jax import lax
from jax.experimental import pallas as pl
from jax.experimental.pallas import tpu as pltpu
from jax.sharding import PartitionSpec as P

SWEEPS = 4
SOFT = 0.001
CUT = 0.02
MESH = pl.DeviceIdType.MESH
VMEM = pl.BlockSpec(memory_space=pltpu.VMEM)
HALF = 8
ROWS = 8
REACH = 3
BELOW = 2
ABOVE = 3
LIMIT = 60 * 1024 * 1024


def element_matrix():
    poisson = 0.3
    lame_first = poisson / ((1.0 + poisson) * (1.0 - 2.0 * poisson))
    lame_shear = 0.5 / (1.0 + poisson)
    elastic = np.zeros((6, 6))
    elastic[:3, :3] = lame_first
    for direction in range(3):
        elastic[direction, direction] += 2.0 * lame_shear
        elastic[direction + 3, direction + 3] = lame_shear
    corner_signs = (
        np.array(
            [
                [a_side, b_side, c_side]
                for a_side in (0, 1)
                for b_side in (0, 1)
                for c_side in (0, 1)
            ]
        )
        * 2.0
        - 1.0
    )
    gauss_points = np.array([-1.0, 1.0]) / np.sqrt(3.0)
    stiffness = np.zeros((24, 24))
    for first_point in gauss_points:
        for second_point in gauss_points:
            for third_point in gauss_points:
                natural = np.array([first_point, second_point, third_point])
                gradients = np.zeros((8, 3))
                for corner in range(8):
                    for direction in range(3):
                        product = corner_signs[corner, direction] / 8.0
                        for other in range(3):
                            if other != direction:
                                product = product * (
                                    1.0 + corner_signs[corner, other] * natural[other]
                                )
                        gradients[corner, direction] = 2.0 * product
                strain = np.zeros((6, 24))
                for corner in range(8):
                    strain[0, corner] = gradients[corner, 0]
                    strain[1, 8 + corner] = gradients[corner, 1]
                    strain[2, 16 + corner] = gradients[corner, 2]
                    strain[3, corner] = gradients[corner, 1]
                    strain[3, 8 + corner] = gradients[corner, 0]
                    strain[4, 8 + corner] = gradients[corner, 2]
                    strain[4, 16 + corner] = gradients[corner, 1]
                    strain[5, corner] = gradients[corner, 2]
                    strain[5, 16 + corner] = gradients[corner, 0]
                stiffness = stiffness + strain.T @ elastic @ strain * 0.125
    return stiffness


def upper_value():
    return 8.0 * float(np.max(np.sum(np.abs(element_matrix()), axis=1)))


def edges():
    upper = upper_value()
    lower = CUT * upper
    return 0.5 * (upper + lower), 0.5 * (upper - lower)


def part_of(offset, size, before, after):
    first = max(offset * size, -before)
    stop = min(offset * size + size, size + after)
    return first - offset * size, first + before, stop - first


def offsets_of(x_size):
    hops = -(-(SWEEPS + REACH) // x_size)
    found = []
    for dx in range(-hops, hops + 1):
        for dy in (-1, 0, 1):
            if (dx, dy) != (0, 0):
                found.append((dx, dy))
    return found


def exchange_kernel(counts, sizes, design, passive, support, warm, d_out, p_out, s_out, w_out, send, recv):
    x_size, y_size = sizes
    gx, yz = lax.axis_index("gx"), lax.axis_index("yz")
    offsets = offsets_of(x_size)
    deep = SWEEPS + REACH

    def there(dx, dy):
        x, y = gx + dx, yz + dy
        return (x >= 0) & (x < counts[0]) & (y >= 0) & (y < counts[1])

    barrier = pltpu.get_barrier_semaphore()
    met = jnp.int32(0)
    for dx, dy in offsets:
        ok = there(dx, dy)
        met = met + ok.astype(jnp.int32)

        @pl.when(ok)
        def _():
            pl.semaphore_signal(barrier, inc=1, device_id=(gx + dx, yz + dy), device_id_type=MESH)

    stride = x_size * y_size
    columns = warm.shape[0] // stride
    for x in range(x_size):
        for y in range(y_size):
            w_out[x + BELOW, y + BELOW] = warm[pl.ds(x * y_size + y, columns, stride=stride), :]
    d_out[deep : deep + x_size, ROWS : ROWS + y_size] = design[...]
    p_out[REACH : REACH + x_size, ROWS : ROWS + y_size] = passive[...]
    s_out[REACH : REACH + x_size, ROWS : ROWS + y_size] = support[...]
    pl.semaphore_wait(barrier, met)

    def copies(dx, dy, slot):
        made = []
        fields = [
            (design, d_out, deep, deep, ROWS, ROWS, False),
            (passive, p_out, REACH, REACH, ROWS, ROWS, False),
            (support, s_out, REACH, REACH, ROWS, ROWS, False),
            (w_out, w_out, BELOW, ABOVE, BELOW, ABOVE, True),
        ]
        for at, (source, target, xb, xa, yb, ya, packed) in enumerate(fields):
            xs, xd, xn = part_of(-dx, x_size, xb, xa)
            ys, yd, yn = part_of(-dy, y_size, yb, ya)
            if xn <= 0 or yn <= 0:
                continue
            if packed:
                xs, ys = xs + BELOW, ys + BELOW
            made.append(
                pltpu.make_async_remote_copy(
                    src_ref=source.at[pl.ds(xs, xn), pl.ds(ys, yn)],
                    dst_ref=target.at[pl.ds(xd, xn), pl.ds(yd, yn)],
                    send_sem=send.at[slot, at],
                    recv_sem=recv.at[slot, at],
                    device_id=(gx + dx, yz + dy),
                    device_id_type=MESH,
                )
            )
        return made

    for slot, (dx, dy) in enumerate(offsets):

        @pl.when(there(dx, dy))
        def _():
            for copy in copies(dx, dy, slot):
                copy.start()

    for slot, (dx, dy) in enumerate(offsets):

        @pl.when(there(-dx, -dy))
        def _():
            for copy in copies(dx, dy, slot):
                copy.wait_recv()

    for slot, (dx, dy) in enumerate(offsets):

        @pl.when(there(dx, dy))
        def _():
            for copy in copies(dx, dy, slot):
                copy.wait_send()


def block_kernel(counts, sizes, modes, d_in, p_in, s_in, w_in, y2_out, scale_out, sums_out, fa, fb, dens, mod, scale, y0, y1, us, ud, fs, fd):
    x_size, y_size = sizes
    depth = d_in.shape[-1]
    x_start, y_start = lax.axis_index("gx") * x_size, lax.axis_index("yz") * y_size
    x_total, y_total = counts[0] * x_size, counts[1] * y_size
    deep = SWEEPS + REACH
    rows = y_size + 2 * ROWS
    row_at = lax.broadcasted_iota(jnp.int32, (rows, depth), 0) + (y_start - ROWS)
    lane_at = lax.broadcasted_iota(jnp.int32, (rows, depth), 1)
    y_in = (row_at >= 0) & (row_at < y_total)
    f32 = jnp.float32

    def one(flag):
        return jnp.where(flag, f32(1.0), f32(0.0))

    yz_part = one(row_at > 0) + one(row_at < y_total - 1) + one(lane_at > 0) + one(lane_at < depth - 1)

    def inside(x):
        return y_in & ((x >= 0) & (x < x_total))

    planes = x_size + 2 * deep

    @pl.loop(0, planes)
    def _(p):
        fa[p] = jnp.where(inside(x_start - deep + p), d_in[p], 0.0)

    for sweep in range(SWEEPS):
        old, new = (fa, fb) if sweep % 2 == 0 else (fb, fa)

        @pl.loop(sweep + 1, planes - sweep - 1)
        def _(p):
            x = x_start - deep + p
            here = old[p]
            around = old[p - 1] + old[p + 1]
            around = around + pltpu.roll(here, 1, 0) + pltpu.roll(here, rows - 1, 0)
            around = around + jnp.where(lane_at > 0, pltpu.roll(here, 1, 1), 0.0)
            around = around + jnp.where(lane_at < depth - 1, pltpu.roll(here, depth - 1, 1), 0.0)
            x_part = jnp.where(x > 0, f32(1.0), f32(0.0)) + jnp.where(x < x_total - 1, f32(1.0), f32(0.0))
            value = (d_in[p] + 2.0 * around) / (1.0 + 2.0 * (x_part + yz_part))
            new[p] = jnp.where(inside(x), value, 0.0)

    last = fa if SWEEPS % 2 == 0 else fb

    @pl.loop(0, x_size + 2 * REACH)
    def _(q):
        x = x_start - REACH + q
        ok = inside(x)
        value = jnp.where(p_in[q] == 1, f32(1.0), last[q + SWEEPS])
        dens[q] = jnp.where(ok, value, 0.0)
        mod[q] = jnp.where(ok, SOFT + (1.0 - SOFT) * (value * value * value), 0.0)

    @pl.loop(1, x_size + 2 * REACH)
    def _(q):
        x = x_start - REACH + q
        pair = dens[q - 1] + dens[q]
        pair = pair + pltpu.roll(pair, 1, 0)
        pair = pair + jnp.where(lane_at > 0, pltpu.roll(pair, 1, 1), 0.0)
        ok = inside(x) & (s_in[q] == 0)
        scale[q] = jnp.where(ok, 1.0 / jnp.sqrt(jnp.where(ok, pair, 8.0) * 0.125), 0.0)

    scale_out[...] = scale[REACH : REACH + x_size, ROWS : ROWS + y_size]

    tile = (HALF, depth)
    lane = lax.broadcasted_iota(jnp.int32, tile, 1)
    sub = lax.broadcasted_iota(jnp.int32, tile, 0)
    x_nodes, y_nodes = x_size + BELOW + ABOVE, y_size + BELOW + ABOVE
    to_row = ROWS - BELOW
    to_plane = REACH - BELOW
    halves = -(-modes // HALF)

    def scale_at(i, j):
        return jnp.broadcast_to(scale[i + to_plane, pl.ds(j + to_row, 1), :], tile)

    def ahead(value):
        return jnp.where(lane < depth - 1, pltpu.roll(value, depth - 1, 1), 0.0)

    def behind(value):
        return jnp.where(lane > 0, pltpu.roll(value, 1, 1), 0.0)

    def put_scaled(h, i, j, c, u):
        after = ahead(u)
        us[h, i, j, c] = u + after
        ud[h, i, j, c] = after - u

    @pl.loop(0, x_nodes)
    def _(i):
        @pl.loop(0, y_nodes)
        def _(j):
            sc = scale_at(i, j)
            for h in range(halves):
                count = min(HALF, modes - h * HALF)
                keep = (sc > 0.0) & (sub < count)
                for c in range(3):
                    first = c * modes + h * HALF
                    begin = min(first, 3 * modes - HALF)
                    value = w_in[i, j, begin : begin + HALF, :]
                    if begin != first:
                        value = pltpu.roll(value, HALF - (first - begin), 0)
                    value = jnp.where(keep, value, 0.0)
                    y0[h, i, j, c] = value
                    put_scaled(h, i, j, c, sc * value)

    poisson = 0.3
    lam = poisson / ((1.0 + poisson) * (1.0 - 2.0 * poisson))
    mu = 0.5 / (1.0 + poisson)
    w0, w1, w2 = 1.0 / 16.0, 1.0 / 48.0, 1.0 / 144.0

    def elements(i0, i1, j0, j1):
        def plane(h, i):
            def x_pairs(j):
                found = []
                for c in range(3):
                    s0, s1 = us[h, i, j, c], us[h, i + 1, j, c]
                    d0, d1 = ud[h, i, j, c], ud[h, i + 1, j, c]
                    found += [s0 + s1, s1 - s0, d0 + d1, d1 - d0]
                return found

            def put(j, part):
                for c in range(3):
                    ss, ds, sd, dd = part[4 * c : 4 * c + 4]
                    fs[h, i, j, c] = fs[h, i, j, c] + (ss - ds)
                    fd[h, i, j, c] = fd[h, i, j, c] + (sd - dd)
                    fs[h, i + 1, j, c] = ss + ds
                    fd[h, i + 1, j, c] = sd + dd

            def column(j, carry):
                low, above = carry[:12], carry[12:]
                high = x_pairs(j + 1)
                e = jnp.broadcast_to(mod[i + to_plane, pl.ds(j + to_row, 1), :], tile)
                u = []
                for c in range(3):
                    now = {}
                    for at, (xb, zb) in enumerate(((0, 0), (1, 0), (0, 1), (1, 1))):
                        p, q = low[4 * c + at], high[4 * c + at]
                        now[xb, 0, zb] = q + p
                        now[xb, 1, zb] = q - p
                    u.append(now)
                a, b, w = u
                fa_, fb_, fw_ = {}, {}, {}
                e_shear = e * (mu * w0)
                e_twice = e * (2.0 * mu * w0)
                x_, y_, z_ = (1, 0, 0), (0, 1, 0), (0, 0, 1)
                xy, xz, yz, xyz = (1, 1, 0), (1, 0, 1), (0, 1, 1), (1, 1, 1)
                trace = (e * (lam * w0)) * (a[x_] + b[y_] + w[z_])
                fa_[x_] = trace + e_twice * a[x_]
                fb_[y_] = trace + e_twice * b[y_]
                fw_[z_] = trace + e_twice * w[z_]
                fa_[y_] = fb_[x_] = e_shear * (a[y_] + b[x_])
                fa_[z_] = fw_[x_] = e_shear * (a[z_] + w[x_])
                fb_[z_] = fw_[y_] = e_shear * (b[z_] + w[y_])
                e_plus = e * ((2.0 * lam + 3.0 * mu) * w1 * 0.5)
                e_minus = e * (3.0 * mu * w1 * 0.5)
                for f1, k1, f2, k2, v1, v2 in (
                    (fa_, xy, fw_, yz, a[xy], w[yz]),
                    (fa_, xz, fb_, yz, a[xz], b[yz]),
                    (fb_, xy, fw_, xz, b[xy], w[xz]),
                ):
                    plus, minus = e_plus * (v1 + v2), e_minus * (v1 - v2)
                    f1[k1], f2[k2] = plus + minus, plus - minus
                e_mixed = e * (mu * w1)
                total = a[yz] + b[xz] + w[xy]
                fa_[yz] = e_mixed * (total + a[yz])
                fb_[xz] = e_mixed * (total + b[xz])
                fw_[xy] = e_mixed * (total + w[xy])
                e_last = e * ((lam + 4.0 * mu) * w2)
                for f, v in ((fa_, a), (fb_, b), (fw_, w)):
                    f[xyz] = e_last * v[xyz]
                part, rest = [], []
                for c, f in enumerate((fa_, fb_, fw_)):
                    for at, (xb, zb) in enumerate(((0, 0), (1, 0), (0, 1), (1, 1))):
                        odd = f[xb, 1, zb]
                        if (xb, zb) == (0, 0):
                            part.append(above[4 * c + at] - odd)
                            rest.append(odd)
                        else:
                            even = f[xb, 0, zb]
                            part.append(above[4 * c + at] + (even - odd))
                            rest.append(even + odd)
                put(j, part)
                return tuple(high) + tuple(rest)

            zero = jnp.zeros(tile, f32)
            carry = lax.fori_loop(j0, j1, column, tuple(x_pairs(j0)) + (zero,) * 12)
            put(j1, carry[12:])

        @pl.loop(0, halves)
        def _(h):
            @pl.loop(j0, j1 + 1)
            def _(j):
                for c in range(3):
                    fs[h, i0, j, c] = jnp.zeros(tile, f32)
                    fd[h, i0, j, c] = jnp.zeros(tile, f32)

            @pl.loop(i0, i1)
            def _(i):
                plane(h, i)

    def force(h, i, j, c):
        s, d = fs[h, i, j, c], fd[h, i, j, c]
        return (s - d) + behind(s + d)

    center, width = edges()
    elements(0, x_nodes - 1, 0, y_nodes - 1)

    @pl.loop(1, x_nodes - 1)
    def _(i):
        @pl.loop(1, y_nodes - 1)
        def _(j):
            sc = scale_at(i, j)
            to = sc * (1.0 / width)
            for h in range(halves):
                for c in range(3):
                    value = to * force(h, i, j, c) - (center / width) * y0[h, i, j, c]
                    y1[h, i, j, c] = value
                    put_scaled(h, i, j, c, sc * value)

    elements(1, x_nodes - 2, 1, y_nodes - 2)

    @pl.loop(BELOW, BELOW + x_size + 1)
    def _(i):
        @pl.loop(BELOW, BELOW + y_size + 1)
        def _(j):
            sc = scale_at(i, j)
            to = sc * (2.0 / width)
            for h in range(halves):
                for c in range(3):
                    value = to * force(h, i, j, c) - (2.0 * center / width) * y1[h, i, j, c] - y0[h, i, j, c]
                    y0[h, i, j, c] = value
                    y1[h, i, j, c] = sc * value
                    put_scaled(h, i, j, c, sc * value)

    elements(BELOW, BELOW + x_size, BELOW, BELOW + y_size)

    y2_out[...] = y0[:, BELOW : BELOW + x_size, BELOW : BELOW + y_size]

    def pairs(i_count, j_count, right, left):
        def body(n, total):
            i, j = BELOW + n // j_count, BELOW + n % j_count
            total = list(total)
            for c in range(3):
                values = [left(h, i, j, c) for h in range(halves)]
                for m in range(modes):
                    other = jnp.broadcast_to(right[m // HALF, i, j, c, m % HALF : m % HALF + 1, :], tile)
                    for h in range(halves):
                        total[m * halves + h] = total[m * halves + h] + values[h] * other
            return tuple(total)

        return lax.fori_loop(0, i_count * j_count, body, (jnp.zeros(tile, f32),) * (modes * halves))

    gram = pairs(x_size, y_size, y0, lambda h, i, j, c: y0[h, i, j, c])
    for h in range(halves):
        out = jnp.zeros(tile, f32)
        for m in range(modes):
            out = jnp.where(lane == m, jnp.sum(gram[m * halves + h], axis=1, keepdims=True), out)
        sums_out[h] = out
    stiff = pairs(x_size + 1, y_size + 1, y1, force)
    for h in range(halves):
        out = sums_out[h]
        for m in range(modes):
            out = jnp.where(lane == 32 + m, jnp.sum(stiff[m * halves + h], axis=1, keepdims=True), out)
        sums_out[h] = out * (1.0 / (3.0 * x_total * y_total * depth))


def sum_kernel(counts, part, out, first, second, send, recv):
    gx, yz = lax.axis_index("gx"), lax.axis_index("yz")
    barrier = pltpu.get_barrier_semaphore()
    x_count, y_count = counts
    for d in range(1, x_count):
        pl.semaphore_signal(barrier, inc=1, device_id=(lax.rem(gx + d, x_count), yz), device_id_type=MESH)
    for d in range(1, y_count):
        pl.semaphore_signal(barrier, inc=1, device_id=(gx, lax.rem(yz + d, y_count)), device_id_type=MESH)
    first[gx] = part[...]
    pl.semaphore_wait(barrier, x_count + y_count - 2)

    def gather(slots, me, count, device, base):
        sent = []
        for d in range(1, count):
            copy = pltpu.make_async_remote_copy(
                src_ref=slots.at[me],
                dst_ref=slots.at[me],
                send_sem=send.at[base + d],
                recv_sem=recv.at[base + d],
                device_id=device(lax.rem(me + d, count)),
                device_id_type=MESH,
            )
            copy.start()
            sent.append(copy)
        for d in range(1, count):
            source = lax.rem(me + count - d, count)
            pltpu.make_async_remote_copy(
                src_ref=slots.at[source],
                dst_ref=slots.at[source],
                send_sem=send.at[base + d],
                recv_sem=recv.at[base + d],
                device_id=device(source),
                device_id_type=MESH,
            ).wait_recv()
        for copy in sent:
            copy.wait_send()
        total = slots[0]
        for k in range(1, count):
            total = total + slots[k]
        return total

    if x_count > 1:
        second[yz] = gather(first, gx, x_count, lambda k: (k, yz), 0)
    else:
        second[yz] = first[0]
    out[...] = gather(second, yz, y_count, lambda k: (gx, k), x_count) if y_count > 1 else second[0]


def finish_kernel(sizes, modes, sums, y2, scale, shapes, projected):
    x_size, y_size = sizes
    depth = y2.shape[-1]
    halves = y2.shape[0]
    rows = halves * HALF
    f32 = jnp.float32
    sub = lax.broadcasted_iota(jnp.int32, (rows, depth), 0)
    lane = lax.broadcasted_iota(jnp.int32, (rows, depth), 1)
    work = sums[...].reshape(rows, depth)
    work = jnp.where((lane < 64) & (sub < modes), work, 0.0)
    work = jnp.where((lane == sub + 64) & (sub < modes), 1.0, work)
    for k in range(modes):
        column = jnp.sum(jnp.where(lane == k, work, 0.0), axis=1, keepdims=True)
        row = work[k : k + 1, :]
        root = 1.0 / jnp.sqrt(column[k : k + 1, :])
        row = row * root
        work = jnp.where(sub == k, row, work - jnp.where(sub > k, column * root, 0.0) * row)
    inverse = jnp.where(lane < modes, pltpu.roll(work, depth - 64, 1), 0.0)
    half_done = jnp.where(lane < modes, pltpu.roll(work, depth - 32, 1), 0.0)
    product = lax.dot_general(
        half_done, inverse, (((1,), (1,)), ((), ())), precision=lax.Precision.HIGHEST, preferred_element_type=f32
    )
    projected[...] = product[:modes, :modes]
    columns = []
    for m in range(modes):
        column = jnp.sum(jnp.where(lane == m, inverse, 0.0), axis=1, keepdims=True)
        for h in range(halves):
            columns.append(jnp.broadcast_to(column[h * HALF : (h + 1) * HALF], (HALF, depth)))
    stride = x_size * y_size

    @pl.loop(0, x_size)
    def _(x):
        @pl.loop(0, y_size)
        def _(y):
            sc = jnp.broadcast_to(scale[x, pl.ds(y, 1), :], (HALF, depth))
            for c in range(3):
                total = [jnp.zeros((HALF, depth), f32)] * halves
                for m in range(modes):
                    one = jnp.broadcast_to(y2[m // HALF, x, y, c, m % HALF : m % HALF + 1, :], (HALF, depth))
                    for h in range(m // HALF, halves):
                        total[h] = total[h] + columns[m * halves + h] * one
                for h in range(halves):
                    count = min(HALF, modes - h * HALF)
                    at = (c * modes + h * HALF) * stride + x * y_size + y
                    shapes[pl.ds(at, count, stride=stride), :] = (sc * total[h])[:count]


def on_device(counts, design, passive, support, warm_modes):
    x_size, y_size, depth = design.shape
    sizes = (x_size, y_size)
    modes = warm_modes.shape[1]
    halves = -(-modes // HALF)
    deep = SWEEPS + REACH
    f32 = jnp.float32
    rows = y_size + 2 * ROWS
    x_nodes, y_nodes = x_size + BELOW + ABOVE, y_size + BELOW + ABOVE
    slots = len(offsets_of(x_size))
    warm = warm_modes.reshape(3 * modes * x_size * y_size, depth)
    extended = pl.pallas_call(
        functools.partial(exchange_kernel, counts, sizes),
        out_shape=(
            jax.ShapeDtypeStruct((x_size + 2 * deep, rows, depth), f32),
            jax.ShapeDtypeStruct((x_size + 2 * REACH, rows, depth), jnp.int32),
            jax.ShapeDtypeStruct((x_size + 2 * REACH, rows, depth), jnp.int32),
            jax.ShapeDtypeStruct((x_nodes, y_nodes, 3 * modes, depth), f32),
        ),
        in_specs=[VMEM] * 4,
        out_specs=(VMEM,) * 4,
        scratch_shapes=[pltpu.SemaphoreType.DMA((slots, 4)), pltpu.SemaphoreType.DMA((slots, 4))],
        compiler_params=pltpu.CompilerParams(collective_id=0, has_side_effects=True, vmem_limit_bytes=LIMIT),
        name="halo_exchange",
    )(design, passive, support, warm)
    block = pltpu.VMEM((halves, x_nodes, y_nodes, 3, HALF, depth), f32)
    field = pltpu.VMEM((x_size + 2 * deep, rows, depth), f32)
    short = pltpu.VMEM((x_size + 2 * REACH, rows, depth), f32)
    y2, scale, sums = pl.pallas_call(
        functools.partial(block_kernel, counts, sizes, modes),
        out_shape=(
            jax.ShapeDtypeStruct((halves, x_size, y_size, 3, HALF, depth), f32),
            jax.ShapeDtypeStruct((x_size, y_size, depth), f32),
            jax.ShapeDtypeStruct((halves, HALF, depth), f32),
        ),
        in_specs=[VMEM] * 4,
        out_specs=(VMEM,) * 3,
        scratch_shapes=[field, field, short, short, short] + [block] * 6,
        compiler_params=pltpu.CompilerParams(vmem_limit_bytes=LIMIT),
        name="filter_block",
    )(*extended)
    total = pl.pallas_call(
        functools.partial(sum_kernel, counts),
        out_shape=jax.ShapeDtypeStruct(sums.shape, f32),
        in_specs=[VMEM],
        out_specs=VMEM,
        scratch_shapes=[
            pltpu.VMEM((counts[0],) + sums.shape, f32),
            pltpu.VMEM((counts[1],) + sums.shape, f32),
            pltpu.SemaphoreType.DMA((counts[0] + counts[1],)),
            pltpu.SemaphoreType.DMA((counts[0] + counts[1],)),
        ],
        compiler_params=pltpu.CompilerParams(collective_id=1, has_side_effects=True),
        name="sum_grams",
    )(sums)
    shapes, projected = pl.pallas_call(
        functools.partial(finish_kernel, sizes, modes),
        out_shape=(
            jax.ShapeDtypeStruct(warm.shape, f32),
            jax.ShapeDtypeStruct((modes, modes), f32),
        ),
        in_specs=[VMEM] * 3,
        out_specs=(VMEM, VMEM),
        compiler_params=pltpu.CompilerParams(vmem_limit_bytes=LIMIT),
        name="orthonormal_shapes",
    )(total, y2, scale)
    return shapes.reshape(warm_modes.shape), projected


def solution(mesh):
    counts = (mesh.shape["gx"], mesh.shape["yz"])
    return jax.shard_map(
        functools.partial(on_device, counts),
        mesh=mesh,
        in_specs=(
            P("gx", "yz", None),
            P("gx", "yz", None),
            P("gx", "yz", None),
            P(None, None, "gx", "yz", None),
        ),
        out_specs=(P(None, None, "gx", "yz", None), P()),
        check_vma=False,
    )
```

time: 537 us -> 141 us (0.26); the launches traced: 527 us -> 141 us
  local copies, waits for them, and re-layouts: 179 us -> 0 us
  Pallas kernels: 0 us -> 140 us
  other arithmetic: 97.1 us -> 0 us
  starting transfers between devices: 93.8 us -> 0 us
  blocking collectives: 52.3 us -> 0 us
  waiting for transfers between devices: 51.1 us -> 0 us
  matrix products: 50.6 us -> 0 us
    pallas_call x0 -> x4, Pallas kernels: none -> 140 us  [the longest x1 86.7 us: on_device(): pl.pallas_call(functools.partial(block_kernel, counts, sizes, modes), out...]
    while x100 -> x0, local copies, waits for them, and re-layouts: 110 us -> none
    ppermute x30 -> x0, starting transfers between devices: 93.8 us -> none  [the longest x14 50.7 us: from_behind(): lax.ppermute(value, axis, [(source, source + steps) for source in range(i...]
    dynamic_update_slice x24 -> x0, other arithmetic: 71.6 us -> none  [add_plane(): lax.dynamic_update_slice_in_dim(accumulated, current + spread[:, :, None]...]
    psum x1 -> x0, blocking collectives: 52.3 us -> none  [on_device(): gram, stiff = lax.psum((gram_part, stiff_part), ('gx', 'yz'))]
    ppermute x30 -> x0, waiting for transfers between devices: 51.1 us -> none  [the longest x14 40.5 us: from_behind(): lax.ppermute(value, axis, [(source, source + steps) for source in range(i...]
    dot_general x17 -> x0, matrix products: 50.4 us -> none  [the longest x12 41.4 us: add_plane(): jnp.einsum('ab,bmyz->amyz', stiffness, gathered, precision=highest_precis...]
    slice x27 -> x0, local copies, waits for them, and re-layouts: 28.9 us -> none  [the longest x12 19.5 us: add_plane(): element_force[:, corner]]
  transfers between devices with their start and end apart: 30 -> 0, of which waited for: 21 -> 0; matrix products, arithmetic and copies ran while one was open for 2% -> 0% of each run, Pallas kernels for 0% -> 0%
where the time goes in v1:
time: 141 us
  Pallas kernels  140 us (99%)
    pallas_call x1, Pallas kernels, on_device(): pl.pallas_call(functools.partial(block_kernel, counts, sizes, modes), out...  86.7 us
    pallas_call x1, Pallas kernels, on_device(): pl.pallas_call(functools.partial(sum_kernel, counts), out_shape=jax.Shape...  30.5 us
    pallas_call x1, Pallas kernels, on_device(): pl.pallas_call(functools.partial(exchange_kernel, counts, sizes), out_sha...  17.2 us
    pallas_call x1, Pallas kernels, on_device(): pl.pallas_call(functools.partial(finish_kernel, sizes, modes), out_shape=...  5.75 us

profile of v1, /device:TPU:0, one launch (start us, length us, event | category | flops | bytes accessed | tf_op | source)
XLA Modules:
  0.0 140.9 jit_solution(6457134572059871009)
XLA Ops:
  0.6 17.2 %halo_exchange.1 = (f32[18,32,128]{2,1,0:T(8,128)}, s32[10,32,128]{2,1,0:T(8,128)}, s32[10,32,128]{2,1,0:T(8,128)}, f32[9,21,36,128]{3,2,1,0:T(8,128)}) custom-call(f32[4,16,128]{2,1,0:T(8,128)} %design.1, s32[4,16,128]{2,1,0:T(8,128)} %passive.1, s32[4,16,128]{2,1,0:T(8,128)} %support.1, f32[2304,128]{1,0:T(8,128)} %bitcast.2), custom_call_target="tpu_custom_call" | custom-call | tf_op jit(solution)/shard_map/halo_exchange/pallas_call | solution.py:550
  17.9 86.7 %filter_block.1 = (f32[2,4,16,3,8,128]{5,4,3,2,1,0:T(8,128)}, f32[4,16,128]{2,1,0:T(8,128)}, f32[2,8,128]{2,1,0:T(8,128)}) custom-call(f32[18,32,128]{2,1,0:T(8,128)} %get-tuple-element.11.d_in, s32[10,32,128]{2,1,0:T(8,128)} %get-tuple-element.12.p_in, s32[10,32,128]{2,1,0:T(8,128)} %get-tuple-element.13.s_in, f32[9,21,36,128]{3,2,1,0:T(8,128)} %get-tuple-element.14.w_in), custom_call_target="tpu_custom_call" | custom-call | tf_op jit(solution)/shard_map/filter_block/pallas_call | solution.py:567
  104.6 30.5 %sum_grams.1.sums = f32[2,8,128]{2,1,0:T(8,128)} custom-call(f32[2,8,128]{2,1,0:T(8,128)} %get-tuple-element.15.part), custom_call_target="tpu_custom_call" | custom-call | tf_op jit(solution)/shard_map/sum_grams/pallas_call | solution.py:580
  135.2 5.8 %orthonormal_shapes.1 = (f32[2304,128]{1,0:T(8,128)}, f32[12,12]{1,0:T(8,128)}) custom-call(f32[2,8,128]{2,1,0:T(8,128)} %sum_grams.1.sums, f32[2,4,16,3,8,128]{5,4,3,2,1,0:T(8,128)} %get-tuple-element.16.y2, f32[4,16,128]{2,1,0:T(8,128)} %get-tuple-element.17.scale), custom_call_target="tpu_custom_call" | custom-call | tf_op jit(solution)/shard_map/orthonormal_shapes/pallas_call | solution.py:594

commit v2 on v1

--- a/solution.py
+++ b/solution.py
@@ -249,7 +249,7 @@
     halves = -(-modes // HALF)
 
     def scale_at(i, j):
-        return jnp.broadcast_to(scale[i + to_plane, pl.ds(j + to_row, 1), :], tile)
+        return jnp.broadcast_to(scale[i + to_plane, j + to_row : j + to_row + 1, :], tile)
 
     def ahead(value):
         return jnp.where(lane < depth - 1, pltpu.roll(value, depth - 1, 1), 0.0)
@@ -264,8 +264,7 @@
 
     @pl.loop(0, x_nodes)
     def _(i):
-        @pl.loop(0, y_nodes)
-        def _(j):
+        for j in range(y_nodes):
             sc = scale_at(i, j)
             for h in range(halves):
                 count = min(HALF, modes - h * HALF)
@@ -306,7 +305,7 @@
             def column(j, carry):
                 low, above = carry[:12], carry[12:]
                 high = x_pairs(j + 1)
-                e = jnp.broadcast_to(mod[i + to_plane, pl.ds(j + to_row, 1), :], tile)
+                e = jnp.broadcast_to(mod[i + to_plane, j + to_row : j + to_row + 1, :], tile)
                 u = []
                 for c in range(3):
                     now = {}
@@ -360,13 +359,14 @@
                 return tuple(high) + tuple(rest)
 
             zero = jnp.zeros(tile, f32)
-            carry = lax.fori_loop(j0, j1, column, tuple(x_pairs(j0)) + (zero,) * 12)
+            carry = tuple(x_pairs(j0)) + (zero,) * 12
+            for j in range(j0, j1):
+                carry = column(j, carry)
             put(j1, carry[12:])
 
         @pl.loop(0, halves)
         def _(h):
-            @pl.loop(j0, j1 + 1)
-            def _(j):
+            for j in range(j0, j1 + 1):
                 for c in range(3):
                     fs[h, i0, j, c] = jnp.zeros(tile, f32)
                     fd[h, i0, j, c] = jnp.zeros(tile, f32)
@@ -384,8 +384,7 @@
 
     @pl.loop(1, x_nodes - 1)
     def _(i):
-        @pl.loop(1, y_nodes - 1)
-        def _(j):
+        for j in range(1, y_nodes - 1):
             sc = scale_at(i, j)
             to = sc * (1.0 / width)
             for h in range(halves):
@@ -398,8 +397,7 @@
 
     @pl.loop(BELOW, BELOW + x_size + 1)
     def _(i):
-        @pl.loop(BELOW, BELOW + y_size + 1)
-        def _(j):
+        for j in range(BELOW, BELOW + y_size + 1):
             sc = scale_at(i, j)
             to = sc * (2.0 / width)
             for h in range(halves):
@@ -433,7 +431,15 @@
         for m in range(modes):
             out = jnp.where(lane == m, jnp.sum(gram[m * halves + h], axis=1, keepdims=True), out)
         sums_out[h] = out
-    stiff = pairs(x_size + 1, y_size + 1, y1, force)
+
+    @pl.loop(BELOW, BELOW + x_size + 1)
+    def _(i):
+        for j in range(BELOW, BELOW + y_size + 1):
+            for h in range(halves):
+                for c in range(3):
+                    us[h, i, j, c] = force(h, i, j, c)
+
+    stiff = pairs(x_size + 1, y_size + 1, y1, lambda h, i, j, c: us[h, i, j, c])
     for h in range(halves):
         out = sums_out[h]
         for m in range(modes):

time: 141 us -> 89.8 us (0.64)
  Pallas kernels: 140 us -> 88.9 us
    pallas_call x1, Pallas kernels: 86.7 us -> 35.4 us  [on_device(): pl.pallas_call(functools.partial(block_kernel, counts, sizes, modes), out...]
where the time goes in v2:
time: 89.8 us; the launch traced here: 89.6 us
  Pallas kernels  88.9 us (99%)
    pallas_call x1, Pallas kernels, on_device(): pl.pallas_call(functools.partial(block_kernel, counts, sizes, modes), out...  35.4 us
    pallas_call x1, Pallas kernels, on_device(): pl.pallas_call(functools.partial(sum_kernel, counts), out_shape=jax.Shape...  30.5 us
    pallas_call x1, Pallas kernels, on_device(): pl.pallas_call(functools.partial(exchange_kernel, counts, sizes), out_sha...  17.2 us
    pallas_call x1, Pallas kernels, on_device(): pl.pallas_call(functools.partial(finish_kernel, sizes, modes), out_shape=...  5.75 us

profile of v2, /device:TPU:0, one launch (start us, length us, event | category | flops | bytes accessed | tf_op | source)
XLA Modules:
  0.0 89.6 jit_solution(1618518415225857625)
XLA Ops:
  0.6 17.2 %halo_exchange.1 = (f32[18,32,128]{2,1,0:T(8,128)}, s32[10,32,128]{2,1,0:T(8,128)}, s32[10,32,128]{2,1,0:T(8,128)}, f32[9,21,36,128]{3,2,1,0:T(8,128)}) custom-call(f32[4,16,128]{2,1,0:T(8,128)} %design.1, s32[4,16,128]{2,1,0:T(8,128)} %passive.1, s32[4,16,128]{2,1,0:T(8,128)} %support.1, f32[2304,128]{1,0:T(8,128)} %bitcast.2), custom_call_target="tpu_custom_call" | custom-call | tf_op jit(solution)/shard_map/halo_exchange/pallas_call | solution.py:556
  17.9 35.4 %filter_block.1 = (f32[2,4,16,3,8,128]{5,4,3,2,1,0:T(8,128)}, f32[4,16,128]{2,1,0:T(8,128)}, f32[2,8,128]{2,1,0:T(8,128)}) custom-call(f32[18,32,128]{2,1,0:T(8,128)} %get-tuple-element.11.d_in, s32[10,32,128]{2,1,0:T(8,128)} %get-tuple-element.12.p_in, s32[10,32,128]{2,1,0:T(8,128)} %get-tuple-element.13.s_in, f32[9,21,36,128]{3,2,1,0:T(8,128)} %get-tuple-element.14.w_in), custom_call_target="tpu_custom_call" | custom-call | tf_op jit(solution)/shard_map/filter_block/pallas_call | solution.py:573
  53.3 30.5 %sum_grams.1.sums = f32[2,8,128]{2,1,0:T(8,128)} custom-call(f32[2,8,128]{2,1,0:T(8,128)} %get-tuple-element.15.part), custom_call_target="tpu_custom_call" | custom-call | tf_op jit(solution)/shard_map/sum_grams/pallas_call | solution.py:586
  83.8 5.8 %orthonormal_shapes.1 = (f32[2304,128]{1,0:T(8,128)}, f32[12,12]{1,0:T(8,128)}) custom-call(f32[2,8,128]{2,1,0:T(8,128)} %sum_grams.1.sums, f32[2,4,16,3,8,128]{5,4,3,2,1,0:T(8,128)} %get-tuple-element.16.y2, f32[4,16,128]{2,1,0:T(8,128)} %get-tuple-element.17.scale), custom_call_target="tpu_custom_call" | custom-call | tf_op jit(solution)/shard_map/orthonormal_shapes/pallas_call | solution.py:600

commit v3 on v2

--- a/solution.py
+++ b/solution.py
@@ -99,86 +99,7 @@
     return found
 
 
-def exchange_kernel(counts, sizes, design, passive, support, warm, d_out, p_out, s_out, w_out, send, recv):
-    x_size, y_size = sizes
-    gx, yz = lax.axis_index("gx"), lax.axis_index("yz")
-    offsets = offsets_of(x_size)
-    deep = SWEEPS + REACH
-
-    def there(dx, dy):
-        x, y = gx + dx, yz + dy
-        return (x >= 0) & (x < counts[0]) & (y >= 0) & (y < counts[1])
-
-    barrier = pltpu.get_barrier_semaphore()
-    met = jnp.int32(0)
-    for dx, dy in offsets:
-        ok = there(dx, dy)
-        met = met + ok.astype(jnp.int32)
-
-        @pl.when(ok)
-        def _():
-            pl.semaphore_signal(barrier, inc=1, device_id=(gx + dx, yz + dy), device_id_type=MESH)
-
-    stride = x_size * y_size
-    columns = warm.shape[0] // stride
-    for x in range(x_size):
-        for y in range(y_size):
-            w_out[x + BELOW, y + BELOW] = warm[pl.ds(x * y_size + y, columns, stride=stride), :]
-    d_out[deep : deep + x_size, ROWS : ROWS + y_size] = design[...]
-    p_out[REACH : REACH + x_size, ROWS : ROWS + y_size] = passive[...]
-    s_out[REACH : REACH + x_size, ROWS : ROWS + y_size] = support[...]
-    pl.semaphore_wait(barrier, met)
-
-    def copies(dx, dy, slot):
-        made = []
-        fields = [
-            (design, d_out, deep, deep, ROWS, ROWS, False),
-            (passive, p_out, REACH, REACH, ROWS, ROWS, False),
-            (support, s_out, REACH, REACH, ROWS, ROWS, False),
-            (w_out, w_out, BELOW, ABOVE, BELOW, ABOVE, True),
-        ]
-        for at, (source, target, xb, xa, yb, ya, packed) in enumerate(fields):
-            xs, xd, xn = part_of(-dx, x_size, xb, xa)
-            ys, yd, yn = part_of(-dy, y_size, yb, ya)
-            if xn <= 0 or yn <= 0:
-                continue
-            if packed:
-                xs, ys = xs + BELOW, ys + BELOW
-            made.append(
-                pltpu.make_async_remote_copy(
-                    src_ref=source.at[pl.ds(xs, xn), pl.ds(ys, yn)],
-                    dst_ref=target.at[pl.ds(xd, xn), pl.ds(yd, yn)],
-                    send_sem=send.at[slot, at],
-                    recv_sem=recv.at[slot, at],
-                    device_id=(gx + dx, yz + dy),
-                    device_id_type=MESH,
-                )
-            )
-        return made
-
-    for slot, (dx, dy) in enumerate(offsets):
-
-        @pl.when(there(dx, dy))
-        def _():
-            for copy in copies(dx, dy, slot):
-                copy.start()
-
-    for slot, (dx, dy) in enumerate(offsets):
-
-        @pl.when(there(-dx, -dy))
-        def _():
-            for copy in copies(dx, dy, slot):
-                copy.wait_recv()
-
-    for slot, (dx, dy) in enumerate(offsets):
-
-        @pl.when(there(dx, dy))
-        def _():
-            for copy in copies(dx, dy, slot):
-                copy.wait_send()
-
-
-def block_kernel(counts, sizes, modes, d_in, p_in, s_in, w_in, y2_out, scale_out, sums_out, fa, fb, dens, mod, scale, y0, y1, us, ud, fs, fd):
+def filter_density(counts, sizes, d_in, p_in, s_in, fa, fb, dens, mod, scale):
     x_size, y_size = sizes
     depth = d_in.shape[-1]
     x_start, y_start = lax.axis_index("gx") * x_size, lax.axis_index("yz") * y_size
@@ -238,15 +159,17 @@
         ok = inside(x) & (s_in[q] == 0)
         scale[q] = jnp.where(ok, 1.0 / jnp.sqrt(jnp.where(ok, pair, 8.0) * 0.125), 0.0)
 
-    scale_out[...] = scale[REACH : REACH + x_size, ROWS : ROWS + y_size]
-
+
+def block_ops(sizes, scale, mod, y0, y1, us, ud, fs, fd):
+    x_size, y_size = sizes
+    depth = scale.shape[-1]
+    f32 = jnp.float32
     tile = (HALF, depth)
     lane = lax.broadcasted_iota(jnp.int32, tile, 1)
     sub = lax.broadcasted_iota(jnp.int32, tile, 0)
     x_nodes, y_nodes = x_size + BELOW + ABOVE, y_size + BELOW + ABOVE
     to_row = ROWS - BELOW
     to_plane = REACH - BELOW
-    halves = -(-modes // HALF)
 
     def scale_at(i, j):
         return jnp.broadcast_to(scale[i + to_plane, j + to_row : j + to_row + 1, :], tile)
@@ -262,29 +185,12 @@
         us[h, i, j, c] = u + after
         ud[h, i, j, c] = after - u
 
-    @pl.loop(0, x_nodes)
-    def _(i):
-        for j in range(y_nodes):
-            sc = scale_at(i, j)
-            for h in range(halves):
-                count = min(HALF, modes - h * HALF)
-                keep = (sc > 0.0) & (sub < count)
-                for c in range(3):
-                    first = c * modes + h * HALF
-                    begin = min(first, 3 * modes - HALF)
-                    value = w_in[i, j, begin : begin + HALF, :]
-                    if begin != first:
-                        value = pltpu.roll(value, HALF - (first - begin), 0)
-                    value = jnp.where(keep, value, 0.0)
-                    y0[h, i, j, c] = value
-                    put_scaled(h, i, j, c, sc * value)
-
     poisson = 0.3
     lam = poisson / ((1.0 + poisson) * (1.0 - 2.0 * poisson))
     mu = 0.5 / (1.0 + poisson)
     w0, w1, w2 = 1.0 / 16.0, 1.0 / 48.0, 1.0 / 144.0
 
-    def elements(i0, i1, j0, j1):
+    def elements(groups, i0, i1, j0, j1):
         def plane(h, i):
             def x_pairs(j):
                 found = []
@@ -364,7 +270,7 @@
                 carry = column(j, carry)
             put(j1, carry[12:])
 
-        @pl.loop(0, halves)
+        @pl.loop(0, groups)
         def _(h):
             for j in range(j0, j1 + 1):
                 for c in range(3):
@@ -379,35 +285,182 @@
         s, d = fs[h, i, j, c], fd[h, i, j, c]
         return (s - d) + behind(s + d)
 
-    center, width = edges()
-    elements(0, x_nodes - 1, 0, y_nodes - 1)
-
-    @pl.loop(1, x_nodes - 1)
-    def _(i):
-        for j in range(1, y_nodes - 1):
-            sc = scale_at(i, j)
-            to = sc * (1.0 / width)
-            for h in range(halves):
+    def filter_modes(groups, count, w_in):
+        @pl.loop(0, x_nodes)
+        def _(i):
+            for j in range(y_nodes):
+                sc = scale_at(i, j)
+                for h in range(groups):
+                    keep = (sc > 0.0) & (sub < count)
+                    for c in range(3):
+                        first = c * count
+                        begin = min(first, 3 * count - HALF)
+                        value = w_in[i, j, begin : begin + HALF, :]
+                        if begin != first:
+                            value = pltpu.roll(value, HALF - (first - begin), 0)
+                        value = jnp.where(keep, value, 0.0)
+                        y0[h, i, j, c] = value
+                        put_scaled(h, i, j, c, sc * value)
+
+        center, width = edges()
+        elements(groups, 0, x_nodes - 1, 0, y_nodes - 1)
+
+        @pl.loop(1, x_nodes - 1)
+        def _(i):
+            for j in range(1, y_nodes - 1):
+                sc = scale_at(i, j)
+                to = sc * (1.0 / width)
+                for h in range(groups):
+                    for c in range(3):
+                        value = to * force(h, i, j, c) - (center / width) * y0[h, i, j, c]
+                        y1[h, i, j, c] = value
+                        put_scaled(h, i, j, c, sc * value)
+
+        elements(groups, 1, x_nodes - 2, 1, y_nodes - 2)
+
+        @pl.loop(BELOW, BELOW + x_size + 1)
+        def _(i):
+            for j in range(BELOW, BELOW + y_size + 1):
+                sc = scale_at(i, j)
+                to = sc * (2.0 / width)
+                for h in range(groups):
+                    for c in range(3):
+                        value = to * force(h, i, j, c) - (2.0 * center / width) * y1[h, i, j, c] - y0[h, i, j, c]
+                        y0[h, i, j, c] = value
+                        y1[h, i, j, c] = sc * value
+                        put_scaled(h, i, j, c, sc * value)
+
+    return filter_modes, elements, force, scale_at, put_scaled
+
+
+def exchange_kernel(counts, sizes, modes, design, passive, support, warm, w_out, mod, scale, y2_out, few, d_out, p_out, s_out, fa, fb, dens, y0, y1, us, ud, fs, fd, send, recv):
+    x_size, y_size = sizes
+    full = modes // HALF * HALF
+    if full == modes:
+        full = modes - HALF
+    rest = modes - full
+    gx, yz = lax.axis_index("gx"), lax.axis_index("yz")
+    offsets = offsets_of(x_size)
+    deep = SWEEPS + REACH
+
+    def there(dx, dy):
+        x, y = gx + dx, yz + dy
+        return (x >= 0) & (x < counts[0]) & (y >= 0) & (y < counts[1])
+
+    barrier = pltpu.get_barrier_semaphore()
+    met = jnp.int32(0)
+    for dx, dy in offsets:
+        ok = there(dx, dy)
+        met = met + ok.astype(jnp.int32)
+
+        @pl.when(ok)
+        def _():
+            pl.semaphore_signal(barrier, inc=1, device_id=(gx + dx, yz + dy), device_id_type=MESH)
+
+    stride = x_size * y_size
+
+    def pack(target, first, count):
+        for x in range(x_size):
+            for y in range(y_size):
                 for c in range(3):
-                    value = to * force(h, i, j, c) - (center / width) * y0[h, i, j, c]
-                    y1[h, i, j, c] = value
-                    put_scaled(h, i, j, c, sc * value)
-
-    elements(1, x_nodes - 2, 1, y_nodes - 2)
+                    begin = (c * modes + first) * stride + x * y_size + y
+                    target[x + BELOW, y + BELOW, c * count : (c + 1) * count] = warm[pl.ds(begin, count, stride=stride), :]
+
+    pack(few, full, rest)
+    d_out[deep : deep + x_size, ROWS : ROWS + y_size] = design[...]
+    p_out[REACH : REACH + x_size, ROWS : ROWS + y_size] = passive[...]
+    s_out[REACH : REACH + x_size, ROWS : ROWS + y_size] = support[...]
+    pl.semaphore_wait(barrier, met)
+
+    def copies(dx, dy, slot, chosen):
+        made = []
+        fields = [
+            (design, d_out, deep, deep, ROWS, ROWS, False),
+            (passive, p_out, REACH, REACH, ROWS, ROWS, False),
+            (support, s_out, REACH, REACH, ROWS, ROWS, False),
+            (few, few, BELOW, ABOVE, BELOW, ABOVE, True),
+            (w_out, w_out, BELOW, ABOVE, BELOW, ABOVE, True),
+        ]
+        for at, (source, target, xb, xa, yb, ya, packed) in enumerate(fields):
+            if at not in chosen:
+                continue
+            xs, xd, xn = part_of(-dx, x_size, xb, xa)
+            ys, yd, yn = part_of(-dy, y_size, yb, ya)
+            if xn <= 0 or yn <= 0:
+                continue
+            if packed:
+                xs, ys = xs + BELOW, ys + BELOW
+            made.append(
+                pltpu.make_async_remote_copy(
+                    src_ref=source.at[pl.ds(xs, xn), pl.ds(ys, yn)],
+                    dst_ref=target.at[pl.ds(xd, xn), pl.ds(yd, yn)],
+                    send_sem=send.at[slot, at],
+                    recv_sem=recv.at[slot, at],
+                    device_id=(gx + dx, yz + dy),
+                    device_id_type=MESH,
+                )
+            )
+        return made
+
+    def start(chosen):
+        for slot, (dx, dy) in enumerate(offsets):
+
+            @pl.when(there(dx, dy))
+            def _():
+                for copy in copies(dx, dy, slot, chosen):
+                    copy.start()
+
+    def arrived(chosen):
+        for slot, (dx, dy) in enumerate(offsets):
+
+            @pl.when(there(-dx, -dy))
+            def _():
+                for copy in copies(dx, dy, slot, chosen):
+                    copy.wait_recv()
+
+    start((0, 1, 2))
+    start((3,))
+    pack(w_out, 0, full)
+    start((4,))
+    arrived((0, 1, 2))
+    filter_density(counts, sizes, d_out, p_out, s_out, fa, fb, dens, mod, scale)
+    arrived((3,))
+    filter_modes = block_ops(sizes, scale, mod, y0, y1, us, ud, fs, fd)[0]
+    filter_modes(1, rest, few)
+    y2_out[...] = y0[0, BELOW : BELOW + x_size + 1, BELOW : BELOW + y_size + 1]
+    arrived((4,))
+    for slot, (dx, dy) in enumerate(offsets):
+
+        @pl.when(there(dx, dy))
+        def _():
+            for copy in copies(dx, dy, slot, (0, 1, 2, 3, 4)):
+                copy.wait_send()
+
+
+def block_kernel(counts, sizes, modes, w_in, mod, scale, y2_in, y2_out, scale_out, sums_out, y0, y1, us, ud, fs, fd):
+    x_size, y_size = sizes
+    depth = scale.shape[-1]
+    f32 = jnp.float32
+    tile = (HALF, depth)
+    lane = lax.broadcasted_iota(jnp.int32, tile, 1)
+    halves = -(-modes // HALF)
+    x_total, y_total = counts[0] * x_size, counts[1] * y_size
+    filter_modes, elements, force, scale_at, put_scaled = block_ops(sizes, scale, mod, y0, y1, us, ud, fs, fd)
+    scale_out[...] = scale[REACH : REACH + x_size, ROWS : ROWS + y_size]
 
     @pl.loop(BELOW, BELOW + x_size + 1)
     def _(i):
         for j in range(BELOW, BELOW + y_size + 1):
             sc = scale_at(i, j)
-            to = sc * (2.0 / width)
-            for h in range(halves):
-                for c in range(3):
-                    value = to * force(h, i, j, c) - (2.0 * center / width) * y1[h, i, j, c] - y0[h, i, j, c]
-                    y0[h, i, j, c] = value
-                    y1[h, i, j, c] = sc * value
-                    put_scaled(h, i, j, c, sc * value)
-
-    elements(BELOW, BELOW + x_size, BELOW, BELOW + y_size)
+            for c in range(3):
+                value = y2_in[i - BELOW, j - BELOW, c]
+                y0[halves - 1, i, j, c] = value
+                y1[halves - 1, i, j, c] = sc * value
+                put_scaled(halves - 1, i, j, c, sc * value)
+
+    if halves > 1:
+        filter_modes(halves - 1, HALF, w_in)
+    elements(halves, BELOW, BELOW + x_size, BELOW, BELOW + y_size)
 
     y2_out[...] = y0[:, BELOW : BELOW + x_size, BELOW : BELOW + y_size]
 
@@ -547,29 +600,42 @@
     sizes = (x_size, y_size)
     modes = warm_modes.shape[1]
     halves = -(-modes // HALF)
+    rest = modes - (halves - 1) * HALF
     deep = SWEEPS + REACH
     f32 = jnp.float32
     rows = y_size + 2 * ROWS
     x_nodes, y_nodes = x_size + BELOW + ABOVE, y_size + BELOW + ABOVE
     slots = len(offsets_of(x_size))
     warm = warm_modes.reshape(3 * modes * x_size * y_size, depth)
-    extended = pl.pallas_call(
-        functools.partial(exchange_kernel, counts, sizes),
+    whole_rows = 3 * (modes - rest)
+    field = pltpu.VMEM((x_size + 2 * deep, rows, depth), f32)
+    short = (x_size + 2 * REACH, rows, depth)
+    one = pltpu.VMEM((1, x_nodes, y_nodes, 3, HALF, depth), f32)
+    block = pltpu.VMEM((halves, x_nodes, y_nodes, 3, HALF, depth), f32)
+    middle = pl.pallas_call(
+        functools.partial(exchange_kernel, counts, sizes, modes),
         out_shape=(
-            jax.ShapeDtypeStruct((x_size + 2 * deep, rows, depth), f32),
-            jax.ShapeDtypeStruct((x_size + 2 * REACH, rows, depth), jnp.int32),
-            jax.ShapeDtypeStruct((x_size + 2 * REACH, rows, depth), jnp.int32),
-            jax.ShapeDtypeStruct((x_nodes, y_nodes, 3 * modes, depth), f32),
+            jax.ShapeDtypeStruct((x_nodes, y_nodes, whole_rows, depth), f32),
+            jax.ShapeDtypeStruct(short, f32),
+            jax.ShapeDtypeStruct(short, f32),
+            jax.ShapeDtypeStruct((x_size + 1, y_size + 1, 3, HALF, depth), f32),
         ),
         in_specs=[VMEM] * 4,
         out_specs=(VMEM,) * 4,
-        scratch_shapes=[pltpu.SemaphoreType.DMA((slots, 4)), pltpu.SemaphoreType.DMA((slots, 4))],
+        scratch_shapes=[
+            pltpu.VMEM((x_nodes, y_nodes, 3 * rest, depth), f32),
+            field,
+            pltpu.VMEM(short, jnp.int32),
+            pltpu.VMEM(short, jnp.int32),
+            field,
+            field,
+            pltpu.VMEM(short, f32),
+        ]
+        + [one] * 6
+        + [pltpu.SemaphoreType.DMA((slots, 5)), pltpu.SemaphoreType.DMA((slots, 5))],
         compiler_params=pltpu.CompilerParams(collective_id=0, has_side_effects=True, vmem_limit_bytes=LIMIT),
-        name="halo_exchange",
+        name="exchange_and_filter",
     )(design, passive, support, warm)
-    block = pltpu.VMEM((halves, x_nodes, y_nodes, 3, HALF, depth), f32)
-    field = pltpu.VMEM((x_size + 2 * deep, rows, depth), f32)
-    short = pltpu.VMEM((x_size + 2 * REACH, rows, depth), f32)
     y2, scale, sums = pl.pallas_call(
         functools.partial(block_kernel, counts, sizes, modes),
         out_shape=(
@@ -579,10 +645,10 @@
         ),
         in_specs=[VMEM] * 4,
         out_specs=(VMEM,) * 3,
-        scratch_shapes=[field, field, short, short, short] + [block] * 6,
+        scratch_shapes=[block] * 6,
         compiler_params=pltpu.CompilerParams(vmem_limit_bytes=LIMIT),
         name="filter_block",
-    )(*extended)
+    )(*middle)
     total = pl.pallas_call(
         functools.partial(sum_kernel, counts),
         out_shape=jax.ShapeDtypeStruct(sums.shape, f32),

time: 89.8 us -> 76.3 us (0.85)
  Pallas kernels: 88.9 us -> 75.4 us
    pallas_call x1, Pallas kernels: 35.4 us -> 22.2 us  [on_device(): pl.pallas_call(functools.partial(block_kernel, counts, sizes, modes), out...]
    pallas_call x1, Pallas kernels: 30.5 us -> 19.7 us  [on_device(): pl.pallas_call(functools.partial(sum_kernel, counts), out_shape=jax.Shape...]
    pallas_call x1, Pallas kernels: 17.2 us -> 27.8 us  [on_device(): pl.pallas_call(functools.partial(exchange_kernel, counts, sizes, modes),...]
where the time goes in v3:
time: 76.3 us; the launch traced here: 76.1 us
  Pallas kernels  75.4 us (99%)
    pallas_call x1, Pallas kernels, on_device(): pl.pallas_call(functools.partial(exchange_kernel, counts, sizes, modes),...  27.8 us
    pallas_call x1, Pallas kernels, on_device(): pl.pallas_call(functools.partial(block_kernel, counts, sizes, modes), out...  22.2 us
    pallas_call x1, Pallas kernels, on_device(): pl.pallas_call(functools.partial(sum_kernel, counts), out_shape=jax.Shape...  19.7 us
    pallas_call x1, Pallas kernels, on_device(): pl.pallas_call(functools.partial(finish_kernel, sizes, modes), out_shape=...  5.75 us

profile of v3, /device:TPU:0, one launch (start us, length us, event | category | flops | bytes accessed | tf_op | source)
XLA Modules:
  0.0 76.1 jit_solution(6773697006569376054)
XLA Ops:
  0.6 27.8 %exchange_and_filter.1 = (f32[9,21,24,128]{3,2,1,0:T(8,128)}, f32[10,32,128]{2,1,0:T(8,128)}, f32[10,32,128]{2,1,0:T(8,128)}, f32[5,17,3,8,128]{4,3,2,1,0:T(8,128)}) custom-call(f32[4,16,128]{2,1,0:T(8,128)} %design.1, s32[4,16,128]{2,1,0:T(8,128)} %passive.1, s32[4,16,128]{2,1,0:T(8,128)} %support.1, f32[2304,128]{1,0:T(8,128)} %bitcast.2), custom_call_target="tpu_custom_call" | custom-call | tf_op jit(solution)/shard_map/exchange_and_filter/pallas_call | solution.py:615
  28.4 22.2 %filter_block.1 = (f32[2,4,16,3,8,128]{5,4,3,2,1,0:T(8,128)}, f32[4,16,128]{2,1,0:T(8,128)}, f32[2,8,128]{2,1,0:T(8,128)}) custom-call(f32[9,21,24,128]{3,2,1,0:T(8,128)} %get-tuple-element.11.w_in, f32[10,32,128]{2,1,0:T(8,128)} %get-tuple-element.12.mod, f32[10,32,128]{2,1,0:T(8,128)} %get-tuple-element.13.scale, f32[5,17,3,8,128]{4,3,2,1,0:T(8,128)} %get-tuple-element.14.y2_in), custom_call_target="tpu_custom_call" | custom-call | tf_op jit(solution)/shard_map/filter_block/pallas_call | solution.py:639
  50.6 19.7 %sum_grams.1.sums = f32[2,8,128]{2,1,0:T(8,128)} custom-call(f32[2,8,128]{2,1,0:T(8,128)} %get-tuple-element.15.part), custom_call_target="tpu_custom_call" | custom-call | tf_op jit(solution)/shard_map/sum_grams/pallas_call | solution.py:652
  70.3 5.8 %orthonormal_shapes.1 = (f32[2304,128]{1,0:T(8,128)}, f32[12,12]{1,0:T(8,128)}) custom-call(f32[2,8,128]{2,1,0:T(8,128)} %sum_grams.1.sums, f32[2,4,16,3,8,128]{5,4,3,2,1,0:T(8,128)} %get-tuple-element.16.y2, f32[4,16,128]{2,1,0:T(8,128)} %get-tuple-element.17.scale), custom_call_target="tpu_custom_call" | custom-call | tf_op jit(solution)/shard_map/orthonormal_shapes/pallas_call | solution.py:666

commit v4 on v3

--- a/solution.py
+++ b/solution.py
@@ -330,10 +330,10 @@
                         y1[h, i, j, c] = sc * value
                         put_scaled(h, i, j, c, sc * value)
 
-    return filter_modes, elements, force, scale_at, put_scaled
-
-
-def exchange_kernel(counts, sizes, modes, design, passive, support, warm, w_out, mod, scale, y2_out, few, d_out, p_out, s_out, fa, fb, dens, y0, y1, us, ud, fs, fd, send, recv):
+    return filter_modes, elements, force
+
+
+def exchange_kernel(counts, sizes, modes, design, passive, support, warm, w_out, mod, scale, y2_out, force_out, few, d_out, p_out, s_out, fa, fb, dens, y0, y1, us, ud, fs, fd, send, recv):
     x_size, y_size = sizes
     full = modes // HALF * HALF
     if full == modes:
@@ -425,9 +425,17 @@
     arrived((0, 1, 2))
     filter_density(counts, sizes, d_out, p_out, s_out, fa, fb, dens, mod, scale)
     arrived((3,))
-    filter_modes = block_ops(sizes, scale, mod, y0, y1, us, ud, fs, fd)[0]
+    filter_modes, elements, force = block_ops(sizes, scale, mod, y0, y1, us, ud, fs, fd)
     filter_modes(1, rest, few)
-    y2_out[...] = y0[0, BELOW : BELOW + x_size + 1, BELOW : BELOW + y_size + 1]
+    elements(1, BELOW, BELOW + x_size, BELOW, BELOW + y_size)
+
+    @pl.loop(0, x_size + 1)
+    def _(i):
+        for j in range(y_size + 1):
+            for c in range(3):
+                y2_out[i, j, c] = y0[0, i + BELOW, j + BELOW, c]
+                force_out[i, j, c] = force(0, i + BELOW, j + BELOW, c)
+
     arrived((4,))
     for slot, (dx, dy) in enumerate(offsets):
 
@@ -437,7 +445,7 @@
                 copy.wait_send()
 
 
-def block_kernel(counts, sizes, modes, w_in, mod, scale, y2_in, y2_out, scale_out, sums_out, y0, y1, us, ud, fs, fd):
+def block_kernel(counts, sizes, modes, w_in, mod, scale, y2_in, force_in, y2_out, scale_out, sums_out, y0, y1, us, ud, fs, fd):
     x_size, y_size = sizes
     depth = scale.shape[-1]
     f32 = jnp.float32
@@ -445,38 +453,40 @@
     lane = lax.broadcasted_iota(jnp.int32, tile, 1)
     halves = -(-modes // HALF)
     x_total, y_total = counts[0] * x_size, counts[1] * y_size
-    filter_modes, elements, force, scale_at, put_scaled = block_ops(sizes, scale, mod, y0, y1, us, ud, fs, fd)
+    filter_modes, elements, force = block_ops(sizes, scale, mod, y0, y1, us, ud, fs, fd)
     scale_out[...] = scale[REACH : REACH + x_size, ROWS : ROWS + y_size]
 
-    @pl.loop(BELOW, BELOW + x_size + 1)
+    @pl.loop(0, x_size + 1)
     def _(i):
-        for j in range(BELOW, BELOW + y_size + 1):
-            sc = scale_at(i, j)
+        for j in range(y_size + 1):
+            at = j + ROWS
+            sc = jnp.broadcast_to(scale[i + REACH, at : at + 1, :], tile)
             for c in range(3):
-                value = y2_in[i - BELOW, j - BELOW, c]
-                y0[halves - 1, i, j, c] = value
-                y1[halves - 1, i, j, c] = sc * value
-                put_scaled(halves - 1, i, j, c, sc * value)
+                value = y2_in[i, j, c]
+                y0[halves - 1, i + BELOW, j + BELOW, c] = value
+                y1[halves - 1, i + BELOW, j + BELOW, c] = sc * value
+                us[halves - 1, i + BELOW, j + BELOW, c] = force_in[i, j, c]
 
     if halves > 1:
         filter_modes(halves - 1, HALF, w_in)
-    elements(halves, BELOW, BELOW + x_size, BELOW, BELOW + y_size)
+    if halves > 1:
+        elements(halves - 1, BELOW, BELOW + x_size, BELOW, BELOW + y_size)
 
     y2_out[...] = y0[:, BELOW : BELOW + x_size, BELOW : BELOW + y_size]
 
     def pairs(i_count, j_count, right, left):
-        def body(n, total):
-            i, j = BELOW + n // j_count, BELOW + n % j_count
+        def body(i, total):
             total = list(total)
-            for c in range(3):
-                values = [left(h, i, j, c) for h in range(halves)]
-                for m in range(modes):
-                    other = jnp.broadcast_to(right[m // HALF, i, j, c, m % HALF : m % HALF + 1, :], tile)
-                    for h in range(halves):
-                        total[m * halves + h] = total[m * halves + h] + values[h] * other
+            for j in range(BELOW, BELOW + j_count):
+                for c in range(3):
+                    values = [left(h, i, j, c) for h in range(halves)]
+                    for m in range(modes):
+                        other = jnp.broadcast_to(right[m // HALF, i, j, c, m % HALF : m % HALF + 1, :], tile)
+                        for h in range(halves):
+                            total[m * halves + h] = total[m * halves + h] + values[h] * other
             return tuple(total)
 
-        return lax.fori_loop(0, i_count * j_count, body, (jnp.zeros(tile, f32),) * (modes * halves))
+        return lax.fori_loop(BELOW, BELOW + i_count, body, (jnp.zeros(tile, f32),) * (modes * halves))
 
     gram = pairs(x_size, y_size, y0, lambda h, i, j, c: y0[h, i, j, c])
     for h in range(halves):
@@ -488,7 +498,7 @@
     @pl.loop(BELOW, BELOW + x_size + 1)
     def _(i):
         for j in range(BELOW, BELOW + y_size + 1):
-            for h in range(halves):
+            for h in range(halves - 1):
                 for c in range(3):
                     us[h, i, j, c] = force(h, i, j, c)
 
@@ -580,9 +590,8 @@
 
     @pl.loop(0, x_size)
     def _(x):
-        @pl.loop(0, y_size)
-        def _(y):
-            sc = jnp.broadcast_to(scale[x, pl.ds(y, 1), :], (HALF, depth))
+        for y in range(y_size):
+            sc = jnp.broadcast_to(scale[x, y : y + 1, :], (HALF, depth))
             for c in range(3):
                 total = [jnp.zeros((HALF, depth), f32)] * halves
                 for m in range(modes):
@@ -619,9 +628,10 @@
             jax.ShapeDtypeStruct(short, f32),
             jax.ShapeDtypeStruct(short, f32),
             jax.ShapeDtypeStruct((x_size + 1, y_size + 1, 3, HALF, depth), f32),
+            jax.ShapeDtypeStruct((x_size + 1, y_size + 1, 3, HALF, depth), f32),
         ),
         in_specs=[VMEM] * 4,
-        out_specs=(VMEM,) * 4,
+        out_specs=(VMEM,) * 5,
         scratch_shapes=[
             pltpu.VMEM((x_nodes, y_nodes, 3 * rest, depth), f32),
             field,
@@ -643,7 +653,7 @@
             jax.ShapeDtypeStruct((x_size, y_size, depth), f32),
             jax.ShapeDtypeStruct((halves, HALF, depth), f32),
         ),
-        in_specs=[VMEM] * 4,
+        in_specs=[VMEM] * 5,
         out_specs=(VMEM,) * 3,
         scratch_shapes=[block] * 6,
         compiler_params=pltpu.CompilerParams(vmem_limit_bytes=LIMIT),

time: 76.3 us -> 73.6 us (0.965)
  Pallas kernels: 75.4 us -> 72.7 us
    pallas_call x1, Pallas kernels: 22.2 us -> 17.9 us  [on_device(): pl.pallas_call(functools.partial(block_kernel, counts, sizes, modes), out...]
    pallas_call x1, Pallas kernels: 27.8 us -> 29.9 us  [on_device(): pl.pallas_call(functools.partial(exchange_kernel, counts, sizes, modes),...]
where the time goes in v4:
time: 73.6 us; the launch traced here: 73.4 us
  Pallas kernels  72.7 us (99%)
    pallas_call x1, Pallas kernels, on_device(): pl.pallas_call(functools.partial(exchange_kernel, counts, sizes, modes),...  29.9 us
    pallas_call x1, Pallas kernels, on_device(): pl.pallas_call(functools.partial(sum_kernel, counts), out_shape=jax.Shape...  19.7 us
    pallas_call x1, Pallas kernels, on_device(): pl.pallas_call(functools.partial(block_kernel, counts, sizes, modes), out...  17.9 us
    pallas_call x1, Pallas kernels, on_device(): pl.pallas_call(functools.partial(finish_kernel, sizes, modes), out_shape=...  5.25 us

profile of v4, /device:TPU:0, one launch (start us, length us, event | category | flops | bytes accessed | tf_op | source)
XLA Modules:
  0.0 73.4 jit_solution(12091496598550104952)
XLA Ops:
  0.6 29.9 %exchange_and_filter.1 = (f32[9,21,24,128]{3,2,1,0:T(8,128)}, f32[10,32,128]{2,1,0:T(8,128)}, f32[10,32,128]{2,1,0:T(8,128)}, f32[5,17,3,8,128]{4,3,2,1,0:T(8,128)}, f32[5,17,3,8,128]{4,3,2,1,0:T(8,128)}) custom-call(f32[4,16,128]{2,1,0:T(8,128)} %design.1, s32[4,16,128]{2,1,0:T(8,128)} %passive.1, s32[4,16,128]{2,1,0:T(8,128)} %support.1, f32[2304,128]{1,0:T(8,128)} %bitcast.2), custom_call_target="tpu_custom_call" | custom-call | tf_op jit(solution)/shard_map/exchange_and_filter/pallas_call | solution.py:624
  30.5 17.9 %filter_block.1 = (f32[2,4,16,3,8,128]{5,4,3,2,1,0:T(8,128)}, f32[4,16,128]{2,1,0:T(8,128)}, f32[2,8,128]{2,1,0:T(8,128)}) custom-call(f32[9,21,24,128]{3,2,1,0:T(8,128)} %get-tuple-element.12.w_in, f32[10,32,128]{2,1,0:T(8,128)} %get-tuple-element.13.mod, f32[10,32,128]{2,1,0:T(8,128)} %get-tuple-element.14.scale, ...), custom_call_target="tpu_custom_call" | custom-call | tf_op jit(solution)/shard_map/filter_block/pallas_call | solution.py:649
  48.4 19.7 %sum_grams.1.sums = f32[2,8,128]{2,1,0:T(8,128)} custom-call(f32[2,8,128]{2,1,0:T(8,128)} %get-tuple-element.17.part), custom_call_target="tpu_custom_call" | custom-call | tf_op jit(solution)/shard_map/sum_grams/pallas_call | solution.py:662
  68.1 5.3 %orthonormal_shapes.1 = (f32[2304,128]{1,0:T(8,128)}, f32[12,12]{1,0:T(8,128)}) custom-call(f32[2,8,128]{2,1,0:T(8,128)} %sum_grams.1.sums, f32[2,4,16,3,8,128]{5,4,3,2,1,0:T(8,128)} %get-tuple-element.18.y2, f32[4,16,128]{2,1,0:T(8,128)} %get-tuple-element.19.scale), custom_call_target="tpu_custom_call" | custom-call | tf_op jit(solution)/shard_map/orthonormal_shapes/pallas_call | solution.py:676

commit v5 on v4

--- a/solution.py
+++ b/solution.py
@@ -372,7 +372,7 @@
     s_out[REACH : REACH + x_size, ROWS : ROWS + y_size] = support[...]
     pl.semaphore_wait(barrier, met)
 
-    def copies(dx, dy, slot, chosen):
+    def copies(dx, dy, slot, chosen, piece=None):
         made = []
         fields = [
             (design, d_out, deep, deep, ROWS, ROWS, False),
@@ -386,6 +386,8 @@
                 continue
             xs, xd, xn = part_of(-dx, x_size, xb, xa)
             ys, yd, yn = part_of(-dy, y_size, yb, ya)
+            if piece is not None:
+                xs, xd, xn = xs + piece, xd + piece, min(1, xn - piece)
             if xn <= 0 or yn <= 0:
                 continue
             if packed:
@@ -410,6 +412,17 @@
                 for copy in copies(dx, dy, slot, chosen):
                     copy.start()
 
+    def start_planes(chosen):
+        order = sorted(enumerate(offsets), key=lambda item: abs(item[1][0]) + abs(item[1][1]))
+        for piece in range(max(x_size, BELOW, ABOVE)):
+            for slot, (dx, dy) in order:
+                if part_of(-dx, x_size, BELOW, ABOVE)[2] > piece:
+
+                    @pl.when(there(dx, dy))
+                    def _():
+                        for copy in copies(dx, dy, slot, chosen, piece):
+                            copy.start()
+
     def arrived(chosen):
         for slot, (dx, dy) in enumerate(offsets):
 
@@ -419,9 +432,9 @@
                     copy.wait_recv()
 
     start((0, 1, 2))
-    start((3,))
+    start_planes((3,))
     pack(w_out, 0, full)
-    start((4,))
+    start_planes((4,))
     arrived((0, 1, 2))
     filter_density(counts, sizes, d_out, p_out, s_out, fa, fb, dens, mod, scale)
     arrived((3,))

time: 73.6 us -> 73.6 us (level)
  no operation moved by 1% of the time
where the time goes in v5:
time: 73.6 us; the launch traced here: 73.4 us
  Pallas kernels  72.7 us (99%)
    pallas_call x1, Pallas kernels, on_device(): pl.pallas_call(functools.partial(exchange_kernel, counts, sizes, modes),...  29.9 us
    pallas_call x1, Pallas kernels, on_device(): pl.pallas_call(functools.partial(sum_kernel, counts), out_shape=jax.Shape...  19.7 us
    pallas_call x1, Pallas kernels, on_device(): pl.pallas_call(functools.partial(block_kernel, counts, sizes, modes), out...  17.9 us
    pallas_call x1, Pallas kernels, on_device(): pl.pallas_call(functools.partial(finish_kernel, sizes, modes), out_shape=...  5.25 us

profile of v5, /device:TPU:0, one launch (start us, length us, event | category | flops | bytes accessed | tf_op | source)
XLA Modules:
  0.0 73.4 jit_solution(3447492128033921010)
XLA Ops:
  0.6 29.9 %exchange_and_filter.1 = (f32[9,21,24,128]{3,2,1,0:T(8,128)}, f32[10,32,128]{2,1,0:T(8,128)}, f32[10,32,128]{2,1,0:T(8,128)}, f32[5,17,3,8,128]{4,3,2,1,0:T(8,128)}, f32[5,17,3,8,128]{4,3,2,1,0:T(8,128)}) custom-call(f32[4,16,128]{2,1,0:T(8,128)} %design.1, s32[4,16,128]{2,1,0:T(8,128)} %passive.1, s32[4,16,128]{2,1,0:T(8,128)} %support.1, f32[2304,128]{1,0:T(8,128)} %bitcast.2), custom_call_target="tpu_custom_call" | custom-call | tf_op jit(solution)/shard_map/exchange_and_filter/pallas_call | solution.py:637
  30.5 17.9 %filter_block.1 = (f32[2,4,16,3,8,128]{5,4,3,2,1,0:T(8,128)}, f32[4,16,128]{2,1,0:T(8,128)}, f32[2,8,128]{2,1,0:T(8,128)}) custom-call(f32[9,21,24,128]{3,2,1,0:T(8,128)} %get-tuple-element.12.w_in, f32[10,32,128]{2,1,0:T(8,128)} %get-tuple-element.13.mod, f32[10,32,128]{2,1,0:T(8,128)} %get-tuple-element.14.scale, ...), custom_call_target="tpu_custom_call" | custom-call | tf_op jit(solution)/shard_map/filter_block/pallas_call | solution.py:662
  48.4 19.7 %sum_grams.1.sums = f32[2,8,128]{2,1,0:T(8,128)} custom-call(f32[2,8,128]{2,1,0:T(8,128)} %get-tuple-element.17.part), custom_call_target="tpu_custom_call" | custom-call | tf_op jit(solution)/shard_map/sum_grams/pallas_call | solution.py:675
  68.1 5.3 %orthonormal_shapes.1 = (f32[2304,128]{1,0:T(8,128)}, f32[12,12]{1,0:T(8,128)}) custom-call(f32[2,8,128]{2,1,0:T(8,128)} %sum_grams.1.sums, f32[2,4,16,3,8,128]{5,4,3,2,1,0:T(8,128)} %get-tuple-element.18.y2, f32[4,16,128]{2,1,0:T(8,128)} %get-tuple-element.19.scale), custom_call_target="tpu_custom_call" | custom-call | tf_op jit(solution)/shard_map/orthonormal_shapes/pallas_call | solution.py:689
